TPU v7x, 512 devices: a whole 4x4x16 slice. The times are simulated.
512 devices in a mesh: member: 64 (over x, z), space: 8 (over y, core).
Axes of the slice: x: 4, y: 4, z: 16, core: 2. Of those that a mesh axis runs over, the one named last changes fastest.
Arguments:
- replica_profiles: float32 [64, 4, 65536], P('member', None, 'space'), may hold values from -6 to 6
- diffusion: float32 [4], replicated, may hold values from 0.04 to 0.16
- velocity: float32 [3, 4], replicated, may hold values from -0.3 to 0.3
- detector_voxel_position: int32 [20480], P(('member', 'space')), may hold values from 14 to 65535, as said below
- detector_quantity_choice: int32 [20480], P(('member', 'space')), may hold values from 0 to 3
- sensor_value: float32 [20480], P(('member', 'space')), may hold values from -48 to 48
- sensor_var: float32 [20480], P(('member', 'space')), may hold values from 80 to 1280
Outputs:
- analysis: float32 [64, 4, 65536], P('member', None, 'space')
Inputs may be any that keep to these rules, and one draw needn't show every extreme that they name: `detector_voxel_position`: A sensor held by the device with member index i and space index j lies in one of the two top layers (z = 14 or 15) of the cells j * 8192 + i * 128 to j * 8192 + i * 128 + 127.
All inputs are finite; a program needn't handle non-finite values.
Results may differ from a plain program's by a relative error of at most 0.00014.
Values sent between devices are 32-bit elements; how exact they have to be, the bound alone decides.
No kernel may reach another device: no remote copies, remote signals or barrier semaphores. Data moves between devices by JAX's collectives and lax.ppermute only.
A program may use at most 64 MiB of HBM per device.

v0:
```python
import jax
import jax.numpy as jnp
from jax import lax
from jax.sharding import PartitionSpec as P

NY = 256
NZ = 16
CX = 2
NS_ITERS = 5


precise_mode = lax.Precision.HIGHEST


def with_halo(cells, sides, width):
    for axis, dim in sides:
        count = lax.axis_size(axis)
        ends = count - 1
        head = lax.slice_in_dim(cells, 0, width, axis=dim)
        tail = lax.slice_in_dim(cells, cells.shape[dim] - width, cells.shape[dim], axis=dim)
        cells = jnp.concatenate(
            [
                lax.ppermute(tail, axis, [(i, (i + 1) % count) for i in range(ends)]),
                cells,
                lax.ppermute(head, axis, [((i + 1) % count, i) for i in range(ends)]),
            ],
            axis=dim,
        )
    return cells


def tendency(
    centre, forward_x, behind_x, forward_y, behind_y, forward_z, behind_z, diffusion, velocity
):
    laplace = (
        forward_x
        + behind_x
        - 2.0 * centre
        + (forward_y + behind_y - 2.0 * centre)
        + (forward_z + behind_z - 2.0 * centre)
    )
    transport = (
        velocity[0] * (forward_x - behind_x)
        + velocity[1] * (forward_y - behind_y)
        + velocity[2] * (forward_z - behind_z)
    )
    return centre + diffusion * laplace - 0.5 * transport


def advance(padded, diffusion, velocity, lane):
    centre = padded[:, 1:-1]
    forward_y = jnp.pad(centre[:, :, NZ:], ((0, 0), (0, 0), (0, NZ)))
    behind_y = jnp.pad(centre[:, :, :-NZ], ((0, 0), (0, 0), (NZ, 0)))
    forward_z = jnp.where(lane != NZ - 1, jnp.pad(centre[:, :, 1:], ((0, 0), (0, 0), (0, 1))), 0.0)
    behind_z = jnp.where(lane != 0, jnp.pad(centre[:, :, :-1], ((0, 0), (0, 0), (1, 0))), 0.0)
    return tendency(
        centre,
        padded[:, 2:],
        padded[:, :-2],
        forward_y,
        behind_y,
        forward_z,
        behind_z,
        diffusion,
        velocity,
    )


def statistics(random_picks, sensor_value, sensor_var):
    sample_mean = jnp.mean(random_picks, axis=0)
    deviation = random_picks - sample_mean
    innovation = sensor_value - sample_mean
    weight = 1.0 / sensor_var
    inner_product_table = jnp.dot(
        deviation * weight, deviation.T, precision=precise_mode, preferred_element_type=jnp.float32
    )
    anomaly_outer_term = jnp.dot(
        deviation, weight * innovation, precision=precise_mode, preferred_element_type=jnp.float32
    )
    return lax.psum((inner_product_table, anomaly_outer_term), ("member", "space"))


def analysis_mixing_coefficients(inner_product_table, anomaly_outer_term):
    members = inner_product_table.shape[0]
    identity = jnp.eye(members, dtype=jnp.float32)
    system = (members - 1.0) * identity + inner_product_table
    scale = jnp.sqrt(jnp.sum(system * system))

    def iterate(counter, carry):
        root, inverse_root = carry
        factor = 0.5 * (3.0 * identity - jnp.dot(inverse_root, root, precision=precise_mode))
        return (
            jnp.dot(root, factor, precision=precise_mode),
            jnp.dot(factor, inverse_root, precision=precise_mode),
        )

    root, inverse_root = lax.fori_loop(0, NS_ITERS, iterate, (system / scale, identity))
    inverse = jnp.dot(inverse_root, inverse_root, precision=precise_mode) / scale
    shift_weights = jnp.dot(inverse, anomaly_outer_term, precision=precise_mode)
    return jnp.sqrt(members - 1.0) * inverse_root / jnp.sqrt(scale) + shift_weights[:, None]


def correct_replicas(member_ensemble, weights):
    centre = jnp.mean(member_ensemble, axis=0)
    anomaly = member_ensemble - centre
    return centre + jnp.einsum("kfc,km->mfc", anomaly, weights, precision=precise_mode)


def per_device(
    replica_profiles,
    diffusion,
    velocity,
    detector_voxel_position,
    detector_quantity_choice,
    sensor_value,
    sensor_var,
):
    quantity_total = replica_profiles.shape[1]
    voxels_in_partition = replica_profiles.shape[2]
    plane_len = NY * NZ
    diffuse = diffusion[:, None, None]
    moving = velocity[:, :, None, None]
    lane = lax.iota(jnp.int32, plane_len) % NZ
    space_index = lax.axis_index("space")
    member_index = lax.axis_index("member")
    member_count = lax.axis_size("member")
    block_len = voxels_in_partition // member_count
    slab_start = space_index * voxels_in_partition
    present_quantity = replica_profiles[0].reshape(quantity_total, CX, plane_len)
    for counter in range(2):
        padded = with_halo(present_quantity, (("space", 1),), 1)
        present_quantity = advance(padded, diffuse, moving, lane)
    predict_replicas = present_quantity.reshape(1, quantity_total, voxels_in_partition)
    member_ensemble = lax.all_to_all(
        predict_replicas, "member", split_axis=2, concat_axis=0, tiled=True
    )
    local_cell = detector_voxel_position - slab_start - member_index * block_len
    random_picks = member_ensemble[:, detector_quantity_choice, local_cell]
    inner_product_table, anomaly_outer_term = statistics(random_picks, sensor_value, sensor_var)
    weights = analysis_mixing_coefficients(inner_product_table, anomaly_outer_term)
    result = correct_replicas(member_ensemble, weights)
    return lax.all_to_all(result, "member", split_axis=0, concat_axis=2, tiled=True)


def solution(mesh):
    in_specs = (
        P("member", None, "space"),
        P(),
        P(),
        P(("member", "space")),
        P(("member", "space")),
        P(("member", "space")),
        P(("member", "space")),
    )
    out_specs = P("member", None, "space")
    return jax.shard_map(
        per_device, mesh=mesh, in_specs=in_specs, out_specs=out_specs, check_vma=False
    )
```

profile of v0, /device:TPU:6, one launch (start us, length us, event | category | flops | bytes accessed | tf_op | source)
XLA Modules:
  0.0 251.2 jit_solution(16320774665722993429)
XLA Ops:
  0.0 0.9 fusion.38
  0.9 1.3 collective-permute-start
  2.2 3.0 %collective-permute-start.1 = (f32[4,1,4096]{2,0,1:T(4,128)S(1)}, f32[4,1,4096]{2,0,1:T(4,128)S(1)}, u32[]{:S(2)}, u32[]{:S(2)}) collective-permute-start(f32[4,1,4096]{2,0,1:T(4,128)S(1)} %get-tuple-element.62), channel_id=1, source_target_pairs={{0,1},{1,2},{2,3},{3,4},{4,5},{5,6},{6,7},{8,9},{9,10},{10,11},{11... | collective-permute-start | bytes 196616 | tf_op jit(solution)/shard_map/ppermute | solution.py:23
  5.2 1.1 fusion.39
  6.3 1.1 fusion.40
  7.5 0.8 slice_bitcast_fusion.2
  8.3 0.0 collective-permute-done
  8.3 0.0 collective-permute-done.1
  8.3 1.3 multiply_subtract_fusion.2
  9.6 0.1 fusion.36
  9.8 1.3 collective-permute-start.2
  11.1 3.7 %collective-permute-start.3 = (f32[4,1,4096]{2,0,1:T(4,128)S(1)}, f32[4,1,4096]{2,0,1:T(4,128)S(1)}, u32[]{:S(2)}, u32[]{:S(2)}) collective-permute-start(f32[4,1,4096]{2,0,1:T(4,128)S(1)} %get-tuple-element.56), channel_id=1, source_target_pairs={{0,1},{1,2},{2,3},{3,4},{4,5},{5,6},{6,7},{8,9},{9,10},{10,11},{11... | collective-permute-start | bytes 196616 | tf_op jit(solution)/shard_map/ppermute | solution.py:23
  14.8 0.1 fusion.37
  14.9 0.0 collective-permute-done.2
  14.9 0.7 collective-permute-done.3
  15.7 1.0 multiply_subtract_fusion
  16.7 6.4 %copy.31 = f32[1,4,8192]{1,0,2:T(1,128)} copy(f32[1,4,8192]{2,1,0:T(4,128)S(1)} %bitcast.74) | data formatting | bytes 262144 | tf_op jit(solution)/shard_map/reshape | solution.py:133
  23.1 0.5 broadcast.109
  23.6 38.3 %reduce.2 = f32[8192,4]{1,0:T(8,128)} reduce(f32[8192,1,4]{2,1,0:T(1,128)} %bitcast.69, f32[]{:T(128)} %broadcast.109), dimensions={1}, to_apply=%bitcast.42.reduce_sub_computation | reduce | bytes 262148
  61.9 0.0 copy-start.2
  61.9 0.0 copy-start
  61.9 0.0 copy-start.1
  61.9 5.8 %reshape.45 = f32[64,1,512]{2,1,0:T(1,128)} reshape(f32[8192,4]{1,0:T(8,128)} %reduce.2) | data formatting | bytes 262144
  67.7 18.8 %all-to-all-start = ((f32[64,1,512]{2,1,0:T(1,128)}), f32[64,1,512]{2,1,0:T(1,128)S(1)}, u32[]{:S(2)}, u32[]{:S(2)}) async-start(f32[64,1,512]{2,1,0:T(1,128)} %reshape.45), calls=%async_computation | async-start | bytes 262144 | tf_op jit(solution)/shard_map/all_to_all | solution.py:134
  86.5 0.0 copy-done.2
  86.5 0.0 copy-done
  86.6 0.0 copy-done.1
  86.6 15.4 %all-to-all-done = f32[64,1,512]{2,1,0:T(1,128)S(1)} async-done(((f32[64,1,512]{2,1,0:T(1,128)}), f32[64,1,512]{2,1,0:T(1,128)S(1)}, u32[]{:S(2)}, u32[]{:S(2)}) %all-to-all-start) | async-done | bytes 131104 | tf_op jit(solution)/shard_map/all_to_all | solution.py:134
  101.9 0.8 reduce.3
  102.8 0.0 copy-start.3
  102.8 8.0 %reshape.46 = f32[8192,1,4]{2,1,0:T(1,128)} reshape(f32[64,512]{1,0:T(8,128)S(1)} %reduce.3) | data formatting | bytes 262144
  110.8 3.7 %copy.33 = f32[64,4,128]{0,2,1:T(8,128)S(1)} copy(f32[64,4,128]{1,2,0:T(8,128)} %bitcast.67) | data formatting | bytes 262144 | tf_op jit(solution)/shard_map/all_to_all | solution.py:134
  114.5 0.9 gather_fusion
  115.4 0.1 reduce_sum.28
  115.5 0.0 copy-done.3
  115.6 0.2 convolution_bitcast_fusion.2
  115.8 0.3 fusion.11
  116.1 101.5 %all-reduce.8 = (f32[64,64]{1,0:T(8,128)S(1)}, f32[64]{0:T(128)S(1)}) all-reduce(f32[64,64]{1,0:T(8,128)S(1)} %fusion.11, f32[64]{0:T(128)S(1)} %convolution_bitcast_fusion.2), channel_id=1, replica_groups=mesh['member'=64,'space'=8] {'member','space'}, use_global_device_ids=true, to_apply=%region_2.3 | all-reduce | flops 4160 | bytes 33280 | tf_op jit(solution)/shard_map/psum | solution.py:80
  217.6 0.6 multiply_reduce_fusion
  218.9 0.1 copy.34
  219.0 3.2 %while.13 = (s32[]{:T(128)}, f32[64,64]{0,1:T(8,128)S(1)}, f32[64,64]{1,0:T(8,128)S(1)}, s32[]{:T(128)}) while((s32[]{:T(128)}, f32[64,64]{0,1:T(8,128)S(1)}, f32[64,64]{1,0:T(8,128)S(1)}, s32[]{:T(128)}) %tuple.34), condition=%wide.region_5.6_spmd.clone, body=%wide.region_4.5_spmd.clone.sunk | while | flops 9453570 | bytes 213045 | solution.py:97
  219.0 0.2 fusion.65
  219.2 0.2 fusion.66
  219.4 0.2 convolution_bitcast_fusion.4
  219.7 0.2 fusion.65
  219.9 0.2 fusion.66
  220.1 0.2 convolution_bitcast_fusion.4
  220.3 0.2 fusion.65
  220.5 0.2 fusion.66
  220.7 0.2 convolution_bitcast_fusion.4
  221.0 0.2 fusion.65
  221.2 0.2 fusion.66
  221.3 0.2 convolution_bitcast_fusion.4
  221.6 0.2 fusion.65
  221.8 0.2 fusion.66
  222.0 0.2 convolution_bitcast_fusion.4
  222.2 0.2 convolution_divide_fusion
  222.4 2.9 %copy.38 = f32[1,4,64,128]{3,2,1,0:T(8,128)S(1)} copy(f32[1,4,64,128]{1,3,2,0:T(8,128)} %bitcast.68) | data formatting | bytes 262144 | tf_op jit(solution)/shard_map/all_to_all | solution.py:134
  225.3 0.1 convolution_bitcast_fusion.1
  225.5 0.4 convolution_add_fusion
  225.9 0.1 copy.36
  226.0 24.6 %all_to_all.36 = f32[64,4,128]{2,1,0:T(4,128)S(1)} all-to-all(f32[64,4,128]{2,1,0:T(4,128)S(1)} %copy.36), channel_id=1, replica_groups=mesh['member'=64,'space'=8] {'member'}, dimensions={0} | all-to-all | bytes 262144 | tf_op jit(solution)/shard_map/all_to_all | solution.py:142
  250.5 0.7 copy.57
  (19 shorter events, 0.1 us)
Async XLA Ops:
  0.9 7.4 %collective-permute-start = (f32[4,1,4096]{2,0,1:T(4,128)S(1)}, f32[4,1,4096]{2,0,1:T(4,128)S(1)}, u32[]{:S(2)}, u32[]{:S(2)}) collective-permute-start(f32[4,1,4096]{2,0,1:T(4,128)S(1)} %get-tuple-element.63), channel_id=1, source_target_pairs={{1,0},{2,1},{3,2},{4,3},{5,4},{6,5},{7,6},{9,8},{10,9},{11,10},{12... | collective-permute-start | bytes 196616 | tf_op jit(solution)/shard_map/ppermute | solution.py:25
  2.2 6.1 %collective-permute-start.1 = (f32[4,1,4096]{2,0,1:T(4,128)S(1)}, f32[4,1,4096]{2,0,1:T(4,128)S(1)}, u32[]{:S(2)}, u32[]{:S(2)}) collective-permute-start(f32[4,1,4096]{2,0,1:T(4,128)S(1)} %get-tuple-element.62), channel_id=1, source_target_pairs={{0,1},{1,2},{2,3},{3,4},{4,5},{5,6},{6,7},{8,9},{9,10},{10,11},{11... | collective-permute-start | bytes 196616 | tf_op jit(solution)/shard_map/ppermute | solution.py:23
  9.8 5.2 %collective-permute-start.2 = (f32[4,1,4096]{2,0,1:T(4,128)S(1)}, f32[4,1,4096]{2,0,1:T(4,128)S(1)}, u32[]{:S(2)}, u32[]{:S(2)}) collective-permute-start(f32[4,1,4096]{2,0,1:T(4,128)S(1)} %get-tuple-element.57), channel_id=1, source_target_pairs={{1,0},{2,1},{3,2},{4,3},{5,4},{6,5},{7,6},{9,8},{10,9},{11,10},{12... | collective-permute-start | bytes 196616 | tf_op jit(solution)/shard_map/ppermute | solution.py:25
  11.1 4.6 %collective-permute-start.3 = (f32[4,1,4096]{2,0,1:T(4,128)S(1)}, f32[4,1,4096]{2,0,1:T(4,128)S(1)}, u32[]{:S(2)}, u32[]{:S(2)}) collective-permute-start(f32[4,1,4096]{2,0,1:T(4,128)S(1)} %get-tuple-element.56), channel_id=1, source_target_pairs={{0,1},{1,2},{2,3},{3,4},{4,5},{5,6},{6,7},{8,9},{9,10},{10,11},{11... | collective-permute-start | bytes 196616 | tf_op jit(solution)/shard_map/ppermute | solution.py:23
  61.9 24.6 %copy-start.2 = (f32[40]{0:T(128)S(1)}, f32[40]{0:T(128)}, u32[]{:S(2)}) copy-start(f32[40]{0:T(128)} %param.15) | copy-start | bytes 484
  61.9 24.7 %copy-start = (s32[40]{0:T(128)S(1)}, s32[40]{0:T(128)}, u32[]{:S(2)}) copy-start(s32[40]{0:T(128)} %param.13) | copy-start | bytes 484
  61.9 24.7 %copy-start.1 = (s32[40]{0:T(128)S(1)}, s32[40]{0:T(128)}, u32[]{:S(2)}) copy-start(s32[40]{0:T(128)} %param.12) | copy-start | bytes 484
  67.7 34.2 %all-to-all-start = ((f32[64,1,512]{2,1,0:T(1,128)}), f32[64,1,512]{2,1,0:T(1,128)S(1)}, u32[]{:S(2)}, u32[]{:S(2)}) async-start(f32[64,1,512]{2,1,0:T(1,128)} %reshape.45), calls=%async_computation | async-start | bytes 262144 | tf_op jit(solution)/shard_map/all_to_all | solution.py:134
  102.8 12.7 %copy-start.3 = (f32[40]{0:T(128)S(1)}, f32[40]{0:T(128)}, u32[]{:S(2)}) copy-start(f32[40]{0:T(128)} %param.14) | copy-start | bytes 484
where the time goes:
time: 252 us; the launch traced here: 251 us
  blocking collectives  126 us (50%)
  other arithmetic  42.3 us (17%)
  local copies, waits for them, and re-layouts  33.2 us (13%)
  starting transfers between devices  28.1 us (11%)
  waiting for transfers between devices  16.1 us (6%)
  matrix products  4.15 us (2%)
    psum x1, blocking collectives, statistics(): lax.psum((inner_product_table, anomaly_outer_term), ('member', 'space'))  101 us
    unnamed x1, other arithmetic  38.3 us
    all_to_all x1, blocking collectives, per_device(): lax.all_to_all(result, 'member', split_axis=0, concat_axis=2, tiled=True)  24.6 us
    all_to_all x1, starting transfers between devices, per_device(): lax.all_to_all(predict_replicas, 'member', split_axis=2, concat_axis=0, t...  18.8 us
    all_to_all x1, waiting for transfers between devices, per_device(): lax.all_to_all(predict_replicas, 'member', split_axis=2, concat_axis=0, t...  15.4 us
    unnamed x13, local copies, waits for them, and re-layouts  15.1 us
    ppermute x2, starting transfers between devices, with_halo(): lax.ppermute(tail, axis, [(i, (i + 1) % count) for i in range(ends)])  6.76 us
    all_to_all x2, local copies, waits for them, and re-layouts, per_device(): lax.all_to_all(predict_replicas, 'member', split_axis=2, concat_axis=0, t...  6.55 us
  transfers between devices with their start and end apart: 5, of which 2 were waited for; matrix products, arithmetic and copies ran while one was open for 1% of the time, Pallas kernels for 0%

commit v1 on v0

v1 whole, which is shorter than its diff:
```python
import functools
import math

import jax
import jax.numpy as jnp
from jax import lax
from jax.experimental import pallas as pl
from jax.experimental.pallas import tpu as pltpu
from jax.sharding import Mesh, PartitionSpec as P

F = 4
NY = 256
NZ = 16
NS_ITERS = 5
MX = 4
MZ = 16
SIDES = 2
MEMBERS = MX * MZ
LANES = 128
PLANE = NY * NZ
CHUNKS = PLANE // LANES
FLAT = 8 * CHUNKS
SUMS = 8 * 7
FLOPS = 10**8
MESSAGE = 2 * F + 1
TABLE = MEMBERS * MEMBERS // 2 // LANES + 1

VMEM = pl.BlockSpec(memory_space=pltpu.VMEM)
SMEM = pl.BlockSpec(memory_space=pltpu.SMEM)
F32 = jnp.float32
MEMBER = ("mx", "mz", "side")
SPACE = ("y", "core")


def call(body, out_shape, in_specs, *operands, flops=None):
    return pl.pallas_call(
        body,
        out_shape=jax.ShapeDtypeStruct(out_shape, F32),
        in_specs=in_specs,
        out_specs=VMEM,
        cost_estimate=flops
        and pl.CostEstimate(flops=flops, bytes_accessed=1 << 18, transcendentals=0),
        compiler_params=pltpu.CompilerParams(vmem_limit_bytes=16 << 20),
    )(*operands)


def in_plane(centre, coef):
    keep, y_next, y_prev, z_next, z_prev = coef
    lane = lax.broadcasted_iota(jnp.int32, centre[0].shape, 1)
    up = [pltpu.roll(tile, LANES - NZ, 1) for tile in centre]
    down = [pltpu.roll(tile, NZ, 1) for tile in centre]
    zero = jnp.zeros_like(centre[0])
    result = []
    for j in range(CHUNKS):
        after = up[j + 1] if j + 1 < CHUNKS else zero
        before = down[j - 1] if j > 0 else zero
        result.append(
            keep * centre[j]
            + y_next * jnp.where(lane < LANES - NZ, up[j], after)
            + y_prev * jnp.where(lane >= NZ, down[j], before)
            + z_next * pltpu.roll(centre[j], LANES - 1, 1)
            + z_prev * pltpu.roll(centre[j], 1, 1)
        )
    return result


def stack(low, high):
    return jnp.concatenate([low, high], axis=0)


def sensor_sums(cell, choice, value, var):
    count = cell.shape[1]
    diagonal = lax.broadcasted_iota(jnp.int32, (count, count), 0) == lax.broadcasted_iota(
        jnp.int32, (count, count), 1
    )

    def column(row):
        return jnp.sum(jnp.where(diagonal, row, 0.0), axis=1, keepdims=True)

    weight = 1.0 / var
    spot = column((cell - 14 + 2 * choice).astype(F32)).astype(jnp.int32)
    lane = lax.broadcasted_iota(jnp.int32, (count, LANES), 1)
    share = jnp.where(spot == lane, column(weight), 0.0)
    share = share + jnp.where(spot + 2 * F == lane, column(weight * value), 0.0)
    return jnp.sum(share, axis=0, keepdims=True)


def early_body(diffusion_ref, velocity_ref, position_ref, choice_ref, value_ref, var_ref, out_ref):
    shape = (2 * F, LANES)
    field = lax.broadcasted_iota(jnp.int32, shape, 0) % F
    inner_z = lax.broadcasted_iota(jnp.int32, shape, 1) % NZ

    def per_field(values):
        tile = jnp.full(shape, values[F - 1], F32)
        for f in range(F - 1):
            tile = jnp.where(field == f, values[f], tile)
        return tile

    diffuse = per_field([diffusion_ref[f] for f in range(F)])
    move = [per_field([0.5 * velocity_ref[a, f] for f in range(F)]) for a in range(3)]
    coef = (
        1.0 - 6.0 * diffuse,
        diffuse - move[1],
        diffuse + move[1],
        jnp.where(inner_z != NZ - 1, diffuse - move[2], 0.0),
        jnp.where(inner_z != 0, diffuse + move[2], 0.0),
        diffuse - move[0],
        diffuse + move[0],
    )
    for i in range(len(coef)):
        out_ref[8 * i : 8 * i + 8, :] = coef[i]
    start = lax.axis_index(SPACE) * (2 * PLANE) + lax.axis_index(MEMBER) * LANES
    out_ref[SUMS : SUMS + 8, :] = jnp.broadcast_to(
        sensor_sums(position_ref[...] - start, choice_ref[...], value_ref[...], var_ref[...]), shape
    )


def own_body(early_ref, own_ref, out_ref):
    own = [stack(own_ref[:, tile(0, j)], own_ref[:, tile(1, j)]) for j in range(CHUNKS)]
    flat = in_plane(own, [early_ref[8 * i : 8 * i + 8, :] for i in range(5)])
    for j in range(CHUNKS):
        out_ref[8 * j : 8 * j + 8, :] = own[j]
        out_ref[FLAT + 8 * j : FLAT + 8 * j + 8, :] = flat[j]


def tile(plane, chunk):
    return slice(plane * PLANE + chunk * LANES, plane * PLANE + (chunk + 1) * LANES)


def forecast_body(early_ref, own_ref, beside_ref, across_ref, out_ref):
    slab = lax.axis_index(SPACE)
    even = slab % 2 == 0
    coef = [early_ref[8 * i : 8 * i + 8, :] for i in range(7)]
    x_next, x_prev = coef[5:]
    own = [own_ref[8 * j : 8 * j + 8, :] for j in range(CHUNKS)]

    def neighbour(first_ref, second_ref, plane, j):
        return jnp.where(even, first_ref[:, tile(plane, j)], second_ref[:, tile(plane, j)])

    left = [[neighbour(across_ref, beside_ref, p, j) for j in range(CHUNKS)] for p in range(2)]
    right = [[neighbour(beside_ref, across_ref, p, j) for j in range(CHUNKS)] for p in range(2)]
    upper = lax.broadcasted_iota(jnp.int32, (2 * F, LANES), 0) >= F
    inside = jnp.where(
        upper,
        jnp.where(slab < lax.axis_size(SPACE) - 1, 1.0, 0.0),
        jnp.where(slab > 0, 1.0, 0.0),
    )
    halo = [stack(left[1][j], right[0][j]) for j in range(CHUNKS)]
    halo_flat = in_plane(halo, coef[:5])
    outer = [
        inside
        * (
            halo_flat[j]
            + x_next * stack(own[j][:F], right[1][j])
            + x_prev * stack(left[0][j], own[j][F:])
        )
        for j in range(CHUNKS)
    ]
    inner = [
        own_ref[FLAT + 8 * j : FLAT + 8 * j + 8, :]
        + x_next * stack(own[j][F:], halo[j][F:])
        + x_prev * stack(halo[j][:F], own[j][:F])
        for j in range(CHUNKS)
    ]
    last = [
        flat + x_next * stack(mid[F:], out[F:]) + x_prev * stack(out[:F], mid[:F])
        for flat, mid, out in zip(in_plane(inner, coef[:5]), inner, outer)
    ]
    lane = lax.broadcasted_iota(jnp.int32, (2 * F, LANES), 1)
    slot = lane % NZ // 2
    packed = []
    for t in range(CHUNKS // 8):
        both = last[8 * t + 7]
        for g in range(7):
            both = jnp.where(slot == g, pltpu.roll(last[8 * t + g], LANES - 14 + 2 * g, 1), both)
        packed.append(both)
    sums = early_ref[SUMS : SUMS + 1, :]
    for p in range(2):
        for half in range(2):
            for z in range(MZ):
                j = half * MZ + z
                top = packed[2 * half + z % SIDES]
                row = (p * CHUNKS + j) * MESSAGE
                out_ref[row : row + F, :] = last[j][p * F : (p + 1) * F]
                out_ref[row + F : row + 2 * F, :] = top[p * F : (p + 1) * F]
                out_ref[row + 2 * F : row + MESSAGE, :] = sums


def halves(x):
    high = x.astype(jnp.bfloat16)
    return high, (x - high.astype(F32)).astype(jnp.bfloat16)


def gram_body(rows_ref, out_ref):
    first = lax.axis_index("mx") * MZ + lax.axis_index("side") * (MZ // SIDES)
    sums = rows_ref[pl.ds(first * MESSAGE + 2 * F, 8, stride=MESSAGE), :]
    lane = lax.broadcasted_iota(jnp.int32, (8, LANES), 1)
    chunk = lax.broadcasted_iota(jnp.int32, (8, LANES), 0)
    own_slot = lane % NZ // 2 == chunk
    moved = sums
    for g in range(1, 8):
        moved = jnp.where(chunk == g, pltpu.roll(sums, 2 * g, 1), moved)

    def spread(slot):
        tile = moved if slot == 0 else pltpu.roll(moved, LANES - 2 * slot, 1)
        return jnp.sum(jnp.where(own_slot, tile, 0.0), axis=0, keepdims=True)

    left, right = [], []
    for f in range(F):
        cells = rows_ref[pl.ds(F + f, MEMBERS, stride=MESSAGE), :]
        mean = jnp.sum(cells, axis=0, keepdims=True) * (1.0 / MEMBERS)
        deviation = cells - mean
        total = spread(f)
        drive = spread(F + f) - total * mean
        last = lax.broadcasted_iota(jnp.int32, (MEMBERS, LANES), 0) == MEMBERS - 1
        left.append(jnp.concatenate(halves(jnp.where(last, drive, deviation * total)), axis=0))
        right.append(jnp.concatenate(halves(deviation), axis=0))
    table = lax.dot_general(
        jnp.concatenate(left, axis=1),
        jnp.concatenate(right, axis=1),
        (((1,), (1,)), ((), ())),
        preferred_element_type=F32,
    )
    table = table[:MEMBERS] + table[MEMBERS:]
    table = table[:, :MEMBERS] + table[:, MEMBERS:]
    half = MEMBERS // 2
    upper, lower = table[:half], table[half:]
    lane = lax.broadcasted_iota(jnp.int32, (half, MEMBERS), 1)
    from_c = lax.broadcasted_iota(jnp.int32, (half, MEMBERS), 0) < lane
    swapped = jnp.concatenate([lower[:, half:], lower[:, :half]], axis=1)
    packed = jnp.where(jnp.logical_and(from_c, lane < half), swapped, upper)
    cross = jnp.concatenate([lower[half - 1 :]] * 2, axis=1)
    packed = jnp.concatenate([packed[: half // 2], packed[half // 2 :]], axis=1)
    out_ref[: TABLE - 1, :] = packed
    out_ref[TABLE - 1 :, :] = jnp.broadcast_to(cross, (out_ref.shape[0] - TABLE + 1, LANES))


def share_body(own_ref, other_ref, out_ref):
    table = own_ref[:TABLE] + other_ref[:TABLE]
    for i in range(out_ref.shape[0] // TABLE):
        out_ref[i * TABLE : (i + 1) * TABLE, :] = table


def mm(a, b):
    a_high, a_low = halves(a)
    b_high, b_low = halves(b)
    dot = functools.partial(jnp.dot, preferred_element_type=F32)
    return dot(a_high, b_high) + (dot(a_high, b_low) + dot(a_low, b_high))


def mix_body(table_ref, rows_ref, out_ref):
    rows = 8 * TABLE
    tables = table_ref[:rows]
    for i in range(1, table_ref.shape[0] // rows):
        tables = tables + table_ref[i * rows : (i + 1) * rows]
    table = tables[:TABLE]
    for i in range(1, 8):
        table = table + tables[i * TABLE : (i + 1) * TABLE]
    square = (MEMBERS, MEMBERS)
    half = MEMBERS // 2
    row = lax.broadcasted_iota(jnp.int32, square, 0)
    lane = lax.broadcasted_iota(jnp.int32, square, 1)
    identity = jnp.where(row == lane, 1.0, 0.0)
    upper = jnp.concatenate([table[: half // 2, :MEMBERS], table[: half // 2, MEMBERS:]], axis=0)
    swapped = jnp.concatenate([upper[:, half:], upper[:, :half]], axis=1)
    both = jnp.concatenate([upper, swapped], axis=0)
    keep = jnp.logical_or(
        jnp.logical_and(row < half, jnp.logical_or(lane >= half, row > lane)),
        jnp.logical_and(row >= half, row < lane),
    )
    off = jnp.where(keep, both, 0.0)
    off = off + jnp.transpose(off)
    diagonal = jnp.where(row < half, both, -jnp.sum(off, axis=1, keepdims=True))
    cross = jnp.sum(identity * table[TABLE - 1 :, :MEMBERS], axis=1, keepdims=True)
    system = jnp.where(row == lane, diagonal + (MEMBERS - 1.0), off)
    scale = jnp.sqrt(jnp.sum(system * system, keepdims=True))

    ensemble = jnp.concatenate(
        [rows_ref[pl.ds(f, MEMBERS, stride=MESSAGE), :] for f in range(F)], axis=1
    )
    centre = jnp.sum(ensemble, axis=0, keepdims=True) * (1.0 / MEMBERS)
    wide = jnp.concatenate(
        [ensemble - centre, jnp.broadcast_to(cross, (MEMBERS, LANES))], axis=1
    )

    root = system / scale
    inverse_root = 1.5 * identity - 0.5 * root
    root = mm(root, inverse_root)
    for step in range(1, NS_ITERS):
        factor = 1.5 * identity - 0.5 * mm(inverse_root, root)
        if step + 1 < NS_ITERS:
            both = mm(jnp.concatenate([root, inverse_root], axis=0), factor)
            root, inverse_root = both[:MEMBERS], both[MEMBERS:]
    wide = mm(factor, mm(inverse_root, wide))
    anomaly, drive = wide[:, : F * LANES], wide[:, F * LANES : F * LANES + 1] / scale
    shift = jnp.sum(drive * anomaly, axis=0, keepdims=True)
    mixed = (centre + shift) + anomaly * (math.sqrt(MEMBERS - 1.0) / jnp.sqrt(scale))
    for f in range(F):
        out_ref[pl.ds(f, MEMBERS, stride=F), :] = mixed[:, f * LANES : (f + 1) * LANES]


def exchange(rows, axes, peers):
    blocks = rows.reshape(peers, -1, 1, LANES)
    return lax.all_to_all(blocks, axes, split_axis=0, concat_axis=0, tiled=True)


def per_device(
    replica_profiles,
    diffusion,
    velocity,
    detector_voxel_position,
    detector_quantity_choice,
    sensor_value,
    sensor_var,
):
    slabs = lax.axis_size(SPACE)
    cells = replica_profiles.shape[2]
    own = replica_profiles.reshape(F, cells)
    pairs = [(i, i + 1) for i in range(0, slabs, 2)]
    beside = lax.ppermute(own, SPACE, pairs + [(b, a) for a, b in pairs])
    pairs = [(i, i + 1) for i in range(1, slabs - 1, 2)]
    across = lax.ppermute(own, SPACE, pairs + [(b, a) for a, b in pairs])
    early = call(
        early_body,
        (SUMS + 8, LANES),
        [SMEM, SMEM] + [VMEM] * 4,
        diffusion,
        velocity,
        detector_voxel_position.reshape(1, -1),
        detector_quantity_choice.reshape(1, -1),
        sensor_value.reshape(1, -1),
        sensor_var.reshape(1, -1),
        flops=FLOPS,
    )
    planes = call(own_body, (2 * FLAT, LANES), [VMEM] * 2, early, own, flops=FLOPS)
    fields = call(
        forecast_body,
        (MEMBERS * MESSAGE, LANES),
        [VMEM] * 4,
        early,
        planes,
        beside,
        across,
        flops=FLOPS,
    )
    rows = exchange(fields, MEMBER, MEMBERS).reshape(MEMBERS * MESSAGE, LANES)
    table = call(gram_body, (24, LANES), [VMEM], rows)
    other = lax.ppermute(table, "core", [(0, 1), (1, 0)])
    group = ("mx", "side", "y")
    peers = lax.axis_size(group)
    table = call(share_body, (peers * TABLE, LANES), [VMEM, VMEM], table, other)
    table = exchange(table, group, peers).reshape(peers * TABLE, LANES)
    mixed = call(mix_body, (MEMBERS * F, LANES), [VMEM, VMEM], table, rows)
    mixed = lax.all_to_all(
        mixed.reshape(MEMBERS, F, LANES), MEMBER, split_axis=0, concat_axis=0, tiled=True
    )
    return mixed.transpose(1, 0, 2).reshape(1, F, cells)


def solution(mesh):
    devices = mesh.devices.reshape(MX, MZ // SIDES, SIDES, -1, 2)
    fine = Mesh(devices, ("mx", "mz", "side", "y", "core"))
    sensors = P(MEMBER + SPACE)
    in_specs = (P(MEMBER, None, SPACE), P(), P(), sensors, sensors, sensors, sensors)
    return jax.shard_map(
        per_device,
        mesh=fine,
        in_specs=in_specs,
        out_specs=P(MEMBER, None, SPACE),
        check_vma=False,
    )
```

time: 252 us -> 91.3 us (0.36)
  blocking collectives: 126 us -> 76.7 us
  other arithmetic: 42.3 us -> 0 us
  local copies, waits for them, and re-layouts: 33.2 us -> 1.55 us
  starting transfers between devices: 28.1 us -> 7.41 us
  waiting for transfers between devices: 16.1 us -> 1.15 us
  matrix products: 4.15 us -> 0 us
  Pallas kernels: 0 us -> 3.98 us
    psum x1 -> x0, blocking collectives: 101 us -> none  [statistics(): lax.psum((inner_product_table, anomaly_outer_term), ('member', 'space'))]
    all_to_all x1 -> x3, blocking collectives: 24.6 us -> 76.7 us  [the longest x2 56.1 us: exchange(): return lax.all_to_all(blocks, axes, split_axis=0, concat_axis=0, tiled=True)]
    unnamed x1 -> x0, other arithmetic: 38.3 us -> none
    all_to_all x1 -> x0, starting transfers between devices: 18.8 us -> none  [per_device(): lax.all_to_all(predict_replicas, 'member', split_axis=2, concat_axis=0, t...]
    all_to_all x1 -> x0, waiting for transfers between devices: 15.4 us -> none  [per_device(): lax.all_to_all(predict_replicas, 'member', split_axis=2, concat_axis=0, t...]
    unnamed x13 -> x15, local copies, waits for them, and re-layouts: 15.1 us -> 1.55 us
    all_to_all x2 -> x0, local copies, waits for them, and re-layouts: 6.55 us -> none  [per_device(): lax.all_to_all(predict_replicas, 'member', split_axis=2, concat_axis=0, t...]
    reshape x1 -> x0, local copies, waits for them, and re-layouts: 6.43 us -> none  [per_device(): present_quantity.reshape(1, quantity_total, voxels_in_partition)]
  transfers between devices with their start and end apart: 5 -> 3, of which waited for: 2 -> 1; matrix products, arithmetic and copies ran while one was open for 1% -> 0% of each run, Pallas kernels for 0% -> 1%
where the time goes in v1:
time: 91.3 us; the launch traced here: 90.9 us
  blocking collectives  76.7 us (84%)
  starting transfers between devices  7.41 us (8%)
  Pallas kernels  3.98 us (4%)
  local copies, waits for them, and re-layouts  1.55 us (2%)
  waiting for transfers between devices  1.15 us (1%)
    all_to_all x2, blocking collectives, exchange(): return lax.all_to_all(blocks, axes, split_axis=0, concat_axis=0, tiled=True)  56.1 us
    all_to_all x1, blocking collectives, per_device(): lax.all_to_all(mixed.reshape(MEMBERS, F, LANES), MEMBER, split_axis=0, co...  20.6 us
    ppermute x1, starting transfers between devices, per_device(): beside = lax.ppermute(own, SPACE, pairs + [(b, a) for a, b in pairs])  4.84 us
    pallas_call x6, Pallas kernels, call(): pl.pallas_call(body, out_shape=jax.ShapeDtypeStruct(out_shape, F32), in_s...  3.98 us
    ppermute x1, starting transfers between devices, per_device(): other = lax.ppermute(table, 'core', [(0, 1), (1, 0)])  1.91 us
  transfers between devices with their start and end apart: 3, of which 1 were waited for; matrix products, arithmetic and copies ran while one was open for 0% of the time, Pallas kernels for 1%

profile of v1, /device:TPU:6, one launch (start us, length us, event | category | flops | bytes accessed | tf_op | source)
XLA Modules:
  0.0 90.9 jit_solution(12186111079070867178)
XLA Ops:
  0.0 0.7 collective-permute-start.1
  0.7 4.8 %collective-permute-start = (f32[4,8192]{1,0:T(4,128)}, f32[4,8192]{1,0:T(4,128)S(1)}, u32[]{:S(2)}, u32[]{:S(2)}) collective-permute-start(f32[4,8192]{1,0:T(4,128)} %bitcast.20), channel_id=1, source_target_pairs={{0,1},{2,3},{4,5},{6,7},{1,0},{3,2},{5,4},{7,6},{8,9},{10,11},{12,... | collective-permute-start | bytes 393224 | tf_op jit(solution)/shard_map/ppermute | solution.py:320
  5.5 0.0 copy-start.5
  5.5 0.0 copy-start.6
  5.5 0.0 copy-start.1
  5.5 0.0 copy-start.2
  5.6 0.0 copy-start.3
  5.6 0.0 copy-start.4
  5.6 0.6 copy-done.5
  6.2 0.0 copy-done.6
  6.2 0.0 copy-done.1
  6.2 0.0 copy-done.2
  6.2 0.0 copy-done.3
  6.2 0.0 copy-done.4
  6.2 0.0 copy-start
  6.2 0.7 shard_map.73.early_ref
  6.9 0.2 copy-done
  7.2 0.2 shard_map.74.own_ref
  7.4 0.0 collective-permute-done.1.across_ref
  7.4 0.0 collective-permute-done.beside_ref
  7.4 0.4 shard_map.75
  7.8 41.0 %all_to_all.15 = f32[64,9,1,128]{3,2,1,0:T(1,128)S(1)} all-to-all(f32[64,9,1,128]{3,2,1,0:T(1,128)S(1)} %bitcast.15), channel_id=1, replica_groups=mesh['mx'=4,'mz'=8,'side'=2,'y'=4,'core'=2] {'mx','mz','side'}, dimensions={0} | all-to-all | bytes 589824 | tf_op jit(solution)/shard_map/all_to_all | solution.py:304
  48.8 0.5 shard_map.76.own_ref
  49.4 1.9 %collective-permute-start.2 = (f32[24,128]{1,0:T(8,128)S(1)}, f32[24,128]{1,0:T(8,128)S(1)}, u32[]{:S(2)}, u32[]{:S(2)}) collective-permute-start(f32[24,128]{1,0:T(8,128)S(1)} %shard_map.76.own_ref), channel_id=1, source_target_pairs={{0,1},{1,0},{2,3},{3,2},{4,5},{5,4},{6,7},{7,6},{8,9},{9,8},{10,11... | collective-permute-start | bytes 36872 | tf_op jit(solution)/shard_map/ppermute | solution.py:348
  51.3 1.1 %collective-permute-done.2.other_ref = f32[24,128]{1,0:T(8,128)S(1)} collective-permute-done((f32[24,128]{1,0:T(8,128)S(1)}, f32[24,128]{1,0:T(8,128)S(1)}, u32[]{:S(2)}, u32[]{:S(2)}) %collective-permute-start.2) | collective-permute-done | bytes 12320 | tf_op jit(solution)/shard_map/ppermute | solution.py:348
  52.5 15.1 %all_to_all.16 = f32[32,17,1,128]{3,2,1,0:T(1,128)S(1)} all-to-all(f32[32,17,1,128]{3,2,1,0:T(1,128)S(1)} %bitcast.16), channel_id=1, replica_groups=mesh['mx'=4,'mz'=8,'side'=2,'y'=4,'core'=2] {'mx','side','y'}, dimensions={0} | all-to-all | bytes 557056 | tf_op jit(solution)/shard_map/all_to_all | solution.py:304
  67.5 2.1 %shard_map.78 = f32[256,128]{1,0:T(8,128)S(1)} custom-call(f32[544,128]{1,0:T(8,128)S(1)} %bitcast.17, f32[576,128]{1,0:T(8,128)S(1)} %bitcast.14), custom_call_target="tpu_custom_call" | custom-call | tf_op jit(solution)/shard_map/pallas_call | solution.py:36
  69.6 20.6 %all_to_all.17 = f32[64,4,128]{2,1,0:T(4,128)S(1)} all-to-all(f32[64,4,128]{2,1,0:T(4,128)S(1)} %bitcast.18), channel_id=1, replica_groups=mesh['mx'=4,'mz'=8,'side'=2,'y'=4,'core'=2] {'mx','mz','side'}, dimensions={0} | all-to-all | bytes 262144 | tf_op jit(solution)/shard_map/all_to_all | solution.py:354
  90.2 0.7 copy.14
  (1 shorter events, 0.0 us)
Async XLA Ops:
  0.0 7.4 %collective-permute-start.1 = (f32[4,8192]{1,0:T(4,128)}, f32[4,8192]{1,0:T(4,128)S(1)}, u32[]{:S(2)}, u32[]{:S(2)}) collective-permute-start(f32[4,8192]{1,0:T(4,128)} %bitcast.19), channel_id=1, source_target_pairs={{1,2},{3,4},{5,6},{2,1},{4,3},{6,5},{9,10},{11,12},{13,14},{10,9},... | collective-permute-start | bytes 393224 | tf_op jit(solution)/shard_map/ppermute | solution.py:322
  0.7 6.7 %collective-permute-start = (f32[4,8192]{1,0:T(4,128)}, f32[4,8192]{1,0:T(4,128)S(1)}, u32[]{:S(2)}, u32[]{:S(2)}) collective-permute-start(f32[4,8192]{1,0:T(4,128)} %bitcast.20), channel_id=1, source_target_pairs={{0,1},{2,3},{4,5},{6,7},{1,0},{3,2},{5,4},{7,6},{8,9},{10,11},{12,... | collective-permute-start | bytes 393224 | tf_op jit(solution)/shard_map/ppermute | solution.py:320
  5.5 0.7 copy-start.5
  5.5 0.7 copy-start.6
  5.5 0.7 copy-start.1
  5.5 0.7 copy-start.2
  5.6 0.7 copy-start.3
  5.6 0.7 copy-start.4
  6.2 0.9 copy-start
  49.4 3.1 %collective-permute-start.2 = (f32[24,128]{1,0:T(8,128)S(1)}, f32[24,128]{1,0:T(8,128)S(1)}, u32[]{:S(2)}, u32[]{:S(2)}) collective-permute-start(f32[24,128]{1,0:T(8,128)S(1)} %shard_map.76.own_ref), channel_id=1, source_target_pairs={{0,1},{1,0},{2,3},{3,2},{4,5},{5,4},{6,7},{7,6},{8,9},{9,8},{10,11... | collective-permute-start | bytes 36872 | tf_op jit(solution)/shard_map/ppermute | solution.py:348

commit v2 on v1

--- a/solution.py
+++ b/solution.py
@@ -1,4 +1,3 @@
-import functools
 import math
 
 import jax
@@ -242,10 +241,13 @@
 
 
 def mm(a, b):
-    a_high, a_low = halves(a)
-    b_high, b_low = halves(b)
-    dot = functools.partial(jnp.dot, preferred_element_type=F32)
-    return dot(a_high, b_high) + (dot(a_high, b_low) + dot(a_low, b_high))
+    product = jnp.dot(
+        jnp.concatenate(halves(a), axis=0),
+        jnp.concatenate(halves(b), axis=0),
+        preferred_element_type=F32,
+    )
+    rows = a.shape[0]
+    return product[:rows] + product[rows:]
 
 
 def mix_body(table_ref, rows_ref, out_ref):
@@ -274,6 +276,7 @@
     cross = jnp.sum(identity * table[TABLE - 1 :, :MEMBERS], axis=1, keepdims=True)
     system = jnp.where(row == lane, diagonal + (MEMBERS - 1.0), off)
     scale = jnp.sqrt(jnp.sum(system * system, keepdims=True))
+    identity, system = (jnp.concatenate([x, x], axis=1) for x in (identity, system))
 
     ensemble = jnp.concatenate(
         [rows_ref[pl.ds(f, MEMBERS, stride=MESSAGE), :] for f in range(F)], axis=1

time: 91.3 us -> 91.1 us (level)
  no operation moved by 1% of the time
where the time goes in v2:
time: 91.1 us; the launch traced here: 90.7 us
  blocking collectives  76.7 us (84%)
  starting transfers between devices  7.41 us (8%)
  Pallas kernels  3.81 us (4%)
  local copies, waits for them, and re-layouts  1.55 us (2%)
  waiting for transfers between devices  1.15 us (1%)
    all_to_all x2, blocking collectives, exchange(): return lax.all_to_all(blocks, axes, split_axis=0, concat_axis=0, tiled=True)  56.1 us
    all_to_all x1, blocking collectives, per_device(): lax.all_to_all(mixed.reshape(MEMBERS, F, LANES), MEMBER, split_axis=0, co...  20.6 us
    ppermute x1, starting transfers between devices, per_device(): beside = lax.ppermute(own, SPACE, pairs + [(b, a) for a, b in pairs])  4.84 us
    pallas_call x6, Pallas kernels, call(): pl.pallas_call(body, out_shape=jax.ShapeDtypeStruct(out_shape, F32), in_s...  3.81 us
    ppermute x1, starting transfers between devices, per_device(): other = lax.ppermute(table, 'core', [(0, 1), (1, 0)])  1.91 us
  transfers between devices with their start and end apart: 3, of which 1 were waited for; matrix products, arithmetic and copies ran while one was open for 0% of the time, Pallas kernels for 1%

profile of v2, /device:TPU:6, one launch (start us, length us, event | category | flops | bytes accessed | tf_op | source)
XLA Modules:
  0.0 90.7 jit_solution(9070007671037275046)
XLA Ops:
  0.0 0.7 collective-permute-start.1
  0.7 4.8 %collective-permute-start = (f32[4,8192]{1,0:T(4,128)}, f32[4,8192]{1,0:T(4,128)S(1)}, u32[]{:S(2)}, u32[]{:S(2)}) collective-permute-start(f32[4,8192]{1,0:T(4,128)} %bitcast.20), channel_id=1, source_target_pairs={{0,1},{2,3},{4,5},{6,7},{1,0},{3,2},{5,4},{7,6},{8,9},{10,11},{12,... | collective-permute-start | bytes 393224 | tf_op jit(solution)/shard_map/ppermute | solution.py:323
  5.5 0.0 copy-start.5
  5.5 0.0 copy-start.6
  5.5 0.0 copy-start.1
  5.5 0.0 copy-start.2
  5.6 0.0 copy-start.3
  5.6 0.0 copy-start.4
  5.6 0.6 copy-done.5
  6.2 0.0 copy-done.6
  6.2 0.0 copy-done.1
  6.2 0.0 copy-done.2
  6.2 0.0 copy-done.3
  6.2 0.0 copy-done.4
  6.2 0.0 copy-start
  6.2 0.7 shard_map.73.early_ref
  6.9 0.2 copy-done
  7.2 0.2 shard_map.74.own_ref
  7.4 0.0 collective-permute-done.1.across_ref
  7.4 0.0 collective-permute-done.beside_ref
  7.4 0.4 shard_map.75
  7.8 41.0 %all_to_all.15 = f32[64,9,1,128]{3,2,1,0:T(1,128)S(1)} all-to-all(f32[64,9,1,128]{3,2,1,0:T(1,128)S(1)} %bitcast.15), channel_id=1, replica_groups=mesh['mx'=4,'mz'=8,'side'=2,'y'=4,'core'=2] {'mx','mz','side'}, dimensions={0} | all-to-all | bytes 589824 | tf_op jit(solution)/shard_map/all_to_all | solution.py:307
  48.8 0.5 shard_map.76.own_ref
  49.4 1.9 %collective-permute-start.2 = (f32[24,128]{1,0:T(8,128)S(1)}, f32[24,128]{1,0:T(8,128)S(1)}, u32[]{:S(2)}, u32[]{:S(2)}) collective-permute-start(f32[24,128]{1,0:T(8,128)S(1)} %shard_map.76.own_ref), channel_id=1, source_target_pairs={{0,1},{1,0},{2,3},{3,2},{4,5},{5,4},{6,7},{7,6},{8,9},{9,8},{10,11... | collective-permute-start | bytes 36872 | tf_op jit(solution)/shard_map/ppermute | solution.py:351
  51.3 1.1 %collective-permute-done.2.other_ref = f32[24,128]{1,0:T(8,128)S(1)} collective-permute-done((f32[24,128]{1,0:T(8,128)S(1)}, f32[24,128]{1,0:T(8,128)S(1)}, u32[]{:S(2)}, u32[]{:S(2)}) %collective-permute-start.2) | collective-permute-done | bytes 12320 | tf_op jit(solution)/shard_map/ppermute | solution.py:351
  52.5 15.1 %all_to_all.16 = f32[32,17,1,128]{3,2,1,0:T(1,128)S(1)} all-to-all(f32[32,17,1,128]{3,2,1,0:T(1,128)S(1)} %bitcast.16), channel_id=1, replica_groups=mesh['mx'=4,'mz'=8,'side'=2,'y'=4,'core'=2] {'mx','side','y'}, dimensions={0} | all-to-all | bytes 557056 | tf_op jit(solution)/shard_map/all_to_all | solution.py:307
  67.5 1.9 %shard_map.78 = f32[256,128]{1,0:T(8,128)S(1)} custom-call(f32[544,128]{1,0:T(8,128)S(1)} %bitcast.17, f32[576,128]{1,0:T(8,128)S(1)} %bitcast.14), custom_call_target="tpu_custom_call" | custom-call | tf_op jit(solution)/shard_map/pallas_call | solution.py:35
  69.5 20.6 %all_to_all.17 = f32[64,4,128]{2,1,0:T(4,128)S(1)} all-to-all(f32[64,4,128]{2,1,0:T(4,128)S(1)} %bitcast.18), channel_id=1, replica_groups=mesh['mx'=4,'mz'=8,'side'=2,'y'=4,'core'=2] {'mx','mz','side'}, dimensions={0} | all-to-all | bytes 262144 | tf_op jit(solution)/shard_map/all_to_all | solution.py:357
  90.1 0.7 copy.14
  (1 shorter events, 0.0 us)
Async XLA Ops:
  0.0 7.4 %collective-permute-start.1 = (f32[4,8192]{1,0:T(4,128)}, f32[4,8192]{1,0:T(4,128)S(1)}, u32[]{:S(2)}, u32[]{:S(2)}) collective-permute-start(f32[4,8192]{1,0:T(4,128)} %bitcast.19), channel_id=1, source_target_pairs={{1,2},{3,4},{5,6},{2,1},{4,3},{6,5},{9,10},{11,12},{13,14},{10,9},... | collective-permute-start | bytes 393224 | tf_op jit(solution)/shard_map/ppermute | solution.py:325
  0.7 6.7 %collective-permute-start = (f32[4,8192]{1,0:T(4,128)}, f32[4,8192]{1,0:T(4,128)S(1)}, u32[]{:S(2)}, u32[]{:S(2)}) collective-permute-start(f32[4,8192]{1,0:T(4,128)} %bitcast.20), channel_id=1, source_target_pairs={{0,1},{2,3},{4,5},{6,7},{1,0},{3,2},{5,4},{7,6},{8,9},{10,11},{12,... | collective-permute-start | bytes 393224 | tf_op jit(solution)/shard_map/ppermute | solution.py:323
  5.5 0.7 copy-start.5
  5.5 0.7 copy-start.6
  5.5 0.7 copy-start.1
  5.5 0.7 copy-start.2
  5.6 0.7 copy-start.3
  5.6 0.7 copy-start.4
  6.2 0.9 copy-start
  49.4 3.1 %collective-permute-start.2 = (f32[24,128]{1,0:T(8,128)S(1)}, f32[24,128]{1,0:T(8,128)S(1)}, u32[]{:S(2)}, u32[]{:S(2)}) collective-permute-start(f32[24,128]{1,0:T(8,128)S(1)} %shard_map.76.own_ref), channel_id=1, source_target_pairs={{0,1},{1,0},{2,3},{3,2},{4,5},{5,4},{6,7},{7,6},{8,9},{9,8},{10,11... | collective-permute-start | bytes 36872 | tf_op jit(solution)/shard_map/ppermute | solution.py:351

commit v3 on v2

--- a/solution.py
+++ b/solution.py
@@ -230,27 +230,12 @@
     packed = jnp.where(jnp.logical_and(from_c, lane < half), swapped, upper)
     cross = jnp.concatenate([lower[half - 1 :]] * 2, axis=1)
     packed = jnp.concatenate([packed[: half // 2], packed[half // 2 :]], axis=1)
-    out_ref[: TABLE - 1, :] = packed
-    out_ref[TABLE - 1 :, :] = jnp.broadcast_to(cross, (out_ref.shape[0] - TABLE + 1, LANES))
-
-
-def share_body(own_ref, other_ref, out_ref):
-    table = own_ref[:TABLE] + other_ref[:TABLE]
     for i in range(out_ref.shape[0] // TABLE):
-        out_ref[i * TABLE : (i + 1) * TABLE, :] = table
-
-
-def mm(a, b):
-    product = jnp.dot(
-        jnp.concatenate(halves(a), axis=0),
-        jnp.concatenate(halves(b), axis=0),
-        preferred_element_type=F32,
-    )
-    rows = a.shape[0]
-    return product[:rows] + product[rows:]
-
-
-def mix_body(table_ref, rows_ref, out_ref):
+        out_ref[i * TABLE : (i + 1) * TABLE - 1, :] = packed
+        out_ref[(i + 1) * TABLE - 1 : (i + 1) * TABLE, :] = cross
+
+
+def table_sum(table_ref):
     rows = 8 * TABLE
     tables = table_ref[:rows]
     for i in range(1, table_ref.shape[0] // rows):
@@ -258,6 +243,27 @@
     table = tables[:TABLE]
     for i in range(1, 8):
         table = table + tables[i * TABLE : (i + 1) * TABLE]
+    return table
+
+
+def share_body(table_ref, out_ref):
+    table = table_sum(table_ref)
+    for i in range(out_ref.shape[0] // TABLE):
+        out_ref[i * TABLE : (i + 1) * TABLE, :] = table
+
+
+def mm(a, b):
+    product = jnp.dot(
+        jnp.concatenate(halves(a), axis=0),
+        jnp.concatenate(halves(b), axis=0),
+        preferred_element_type=F32,
+    )
+    rows = a.shape[0]
+    return product[:rows] + product[rows:]
+
+
+def mix_body(table_ref, rows_ref, out_ref):
+    table = table_sum(table_ref)
     square = (MEMBERS, MEMBERS)
     half = MEMBERS // 2
     row = lax.broadcasted_iota(jnp.int32, square, 0)
@@ -347,11 +353,11 @@
         flops=FLOPS,
     )
     rows = exchange(fields, MEMBER, MEMBERS).reshape(MEMBERS * MESSAGE, LANES)
-    table = call(gram_body, (24, LANES), [VMEM], rows)
-    other = lax.ppermute(table, "core", [(0, 1), (1, 0)])
-    group = ("mx", "side", "y")
+    table = call(gram_body, (slabs * TABLE, LANES), [VMEM], rows)
+    table = exchange(table, SPACE, slabs).reshape(slabs * TABLE, LANES)
+    group = ("mx", "side")
     peers = lax.axis_size(group)
-    table = call(share_body, (peers * TABLE, LANES), [VMEM, VMEM], table, other)
+    table = call(share_body, (peers * TABLE, LANES), [VMEM], table)
     table = exchange(table, group, peers).reshape(peers * TABLE, LANES)
     mixed = call(mix_body, (MEMBERS * F, LANES), [VMEM, VMEM], table, rows)
     mixed = lax.all_to_all(

time: 91.1 us -> 91.5 us (level)
  blocking collectives: 76.7 us -> 80.1 us
  starting transfers between devices: 7.41 us -> 5.5 us
  waiting for transfers between devices: 1.15 us -> 0.01 us
    all_to_all x2 -> x3, blocking collectives: 56.1 us -> 59.8 us  [exchange(): return lax.all_to_all(blocks, axes, split_axis=0, concat_axis=0, tiled=True)]
    ppermute x1 -> x0, starting transfers between devices: 1.91 us -> none  [per_device(): other = lax.ppermute(table, 'core', [(0, 1), (1, 0)])]
    ppermute x1 -> x0, waiting for transfers between devices: 1.14 us -> none  [per_device(): other = lax.ppermute(table, 'core', [(0, 1), (1, 0)])]
  transfers between devices with their start and end apart: 3 -> 2, of which waited for: 1 -> 0; matrix products, arithmetic and copies ran while one was open for 0% -> 0% of each run, Pallas kernels for 1% -> 1%
where the time goes in v3:
time: 91.5 us; the launch traced here: 91.1 us
  blocking collectives  80.1 us (88%)
  starting transfers between devices  5.5 us (6%)
  Pallas kernels  3.81 us (4%)
  local copies, waits for them, and re-layouts  1.55 us (2%)
    all_to_all x3, blocking collectives, exchange(): return lax.all_to_all(blocks, axes, split_axis=0, concat_axis=0, tiled=True)  59.8 us
    all_to_all x1, blocking collectives, per_device(): lax.all_to_all(mixed.reshape(MEMBERS, F, LANES), MEMBER, split_axis=0, co...  20.4 us
    ppermute x1, starting transfers between devices, per_device(): beside = lax.ppermute(own, SPACE, pairs + [(b, a) for a, b in pairs])  4.84 us
    pallas_call x6, Pallas kernels, call(): pl.pallas_call(body, out_shape=jax.ShapeDtypeStruct(out_shape, F32), in_s...  3.81 us
  transfers between devices with their start and end apart: 2, of which 0 were waited for; matrix products, arithmetic and copies ran while one was open for 0% of the time, Pallas kernels for 1%

profile of v3, /device:TPU:6, one launch (start us, length us, event | category | flops | bytes accessed | tf_op | source)
XLA Modules:
  0.0 91.1 jit_solution(12249280823963598681)
XLA Ops:
  0.0 0.7 collective-permute-start.1
  0.7 4.8 %collective-permute-start = (f32[4,8192]{1,0:T(4,128)}, f32[4,8192]{1,0:T(4,128)S(1)}, u32[]{:S(2)}, u32[]{:S(2)}) collective-permute-start(f32[4,8192]{1,0:T(4,128)} %bitcast.24), channel_id=1, source_target_pairs={{0,1},{2,3},{4,5},{6,7},{1,0},{3,2},{5,4},{7,6},{8,9},{10,11},{12,... | collective-permute-start | bytes 393224 | tf_op jit(solution)/shard_map/ppermute | solution.py:329
  5.5 0.0 copy-start.5
  5.5 0.0 copy-start.6
  5.5 0.0 copy-start.1
  5.5 0.0 copy-start.2
  5.6 0.0 copy-start.3
  5.6 0.0 copy-start.4
  5.6 0.6 copy-done.5
  6.2 0.0 copy-done.6
  6.2 0.0 copy-done.1
  6.2 0.0 copy-done.2
  6.2 0.0 copy-done.3
  6.2 0.0 copy-done.4
  6.2 0.0 copy-start
  6.2 0.7 shard_map.73.early_ref
  6.9 0.2 copy-done
  7.2 0.2 shard_map.74.own_ref
  7.4 0.0 collective-permute-done.1.across_ref
  7.4 0.0 collective-permute-done.beside_ref
  7.4 0.5 shard_map.75
  7.8 41.0 %all_to_all.20 = f32[64,9,1,128]{3,2,1,0:T(1,128)S(1)} all-to-all(f32[64,9,1,128]{3,2,1,0:T(1,128)S(1)} %bitcast.17), channel_id=1, replica_groups=mesh['mx'=4,'mz'=8,'side'=2,'y'=4,'core'=2] {'mx','mz','side'}, dimensions={0} | all-to-all | bytes 589824 | tf_op jit(solution)/shard_map/all_to_all | solution.py:313
  48.8 0.5 shard_map.76
  49.4 9.6 %all_to_all.21 = f32[8,17,1,128]{3,2,1,0:T(1,128)S(1)} all-to-all(f32[8,17,1,128]{3,2,1,0:T(1,128)S(1)} %bitcast.21), channel_id=1, replica_groups=mesh['mx'=4,'mz'=8,'side'=2,'y'=4,'core'=2] {'y','core'}, dimensions={0} | all-to-all | bytes 139264 | tf_op jit(solution)/shard_map/all_to_all | solution.py:313
  59.0 9.1 %all_to_all.22 = f32[8,17,1,128]{3,2,1,0:T(1,128)S(1)} all-to-all(f32[8,17,1,128]{3,2,1,0:T(1,128)S(1)} %bitcast.20), channel_id=1, replica_groups=mesh['mx'=4,'mz'=8,'side'=2,'y'=4,'core'=2] {'mx','side'}, dimensions={0} | all-to-all | bytes 139264 | tf_op jit(solution)/shard_map/all_to_all | solution.py:313
  68.1 1.9 %shard_map.78 = f32[256,128]{1,0:T(8,128)S(1)} custom-call(f32[136,128]{1,0:T(8,128)S(1)} %bitcast.22, f32[576,128]{1,0:T(8,128)S(1)} %bitcast.16), custom_call_target="tpu_custom_call" | custom-call | tf_op jit(solution)/shard_map/pallas_call | solution.py:35
  70.1 20.4 %all_to_all.23 = f32[64,4,128]{2,1,0:T(4,128)S(1)} all-to-all(f32[64,4,128]{2,1,0:T(4,128)S(1)} %bitcast.18), channel_id=1, replica_groups=mesh['mx'=4,'mz'=8,'side'=2,'y'=4,'core'=2] {'mx','mz','side'}, dimensions={0} | all-to-all | bytes 262144 | tf_op jit(solution)/shard_map/all_to_all | solution.py:363
  90.4 0.7 copy.15
  (1 shorter events, 0.0 us)
Async XLA Ops:
  0.0 7.4 %collective-permute-start.1 = (f32[4,8192]{1,0:T(4,128)}, f32[4,8192]{1,0:T(4,128)S(1)}, u32[]{:S(2)}, u32[]{:S(2)}) collective-permute-start(f32[4,8192]{1,0:T(4,128)} %bitcast.23), channel_id=1, source_target_pairs={{1,2},{3,4},{5,6},{2,1},{4,3},{6,5},{9,10},{11,12},{13,14},{10,9},... | collective-permute-start | bytes 393224 | tf_op jit(solution)/shard_map/ppermute | solution.py:331
  0.7 6.7 %collective-permute-start = (f32[4,8192]{1,0:T(4,128)}, f32[4,8192]{1,0:T(4,128)S(1)}, u32[]{:S(2)}, u32[]{:S(2)}) collective-permute-start(f32[4,8192]{1,0:T(4,128)} %bitcast.24), channel_id=1, source_target_pairs={{0,1},{2,3},{4,5},{6,7},{1,0},{3,2},{5,4},{7,6},{8,9},{10,11},{12,... | collective-permute-start | bytes 393224 | tf_op jit(solution)/shard_map/ppermute | solution.py:329
  5.5 0.7 copy-start.5
  5.5 0.7 copy-start.6
  5.5 0.7 copy-start.1
  5.5 0.7 copy-start.2
  5.6 0.7 copy-start.3
  5.6 0.7 copy-start.4
  6.2 0.9 copy-start

commit v4 on v2

--- a/solution.py
+++ b/solution.py
@@ -228,7 +228,11 @@
     from_c = lax.broadcasted_iota(jnp.int32, (half, MEMBERS), 0) < lane
     swapped = jnp.concatenate([lower[:, half:], lower[:, :half]], axis=1)
     packed = jnp.where(jnp.logical_and(from_c, lane < half), swapped, upper)
-    cross = jnp.concatenate([lower[half - 1 :]] * 2, axis=1)
+    on_diagonal = lax.broadcasted_iota(jnp.int32, (half, MEMBERS), 0) + half == lane
+    diagonal = jnp.sum(jnp.where(on_diagonal, lower, 0.0), axis=0, keepdims=True)
+    last = -jnp.sum(upper, axis=0, keepdims=True) - jnp.sum(lower[: half - 1], axis=0, keepdims=True)
+    diagonal = jnp.where(lane[:1] == MEMBERS - 1, last, diagonal)
+    cross = jnp.concatenate([lower[half - 1 :], diagonal], axis=1)
     packed = jnp.concatenate([packed[: half // 2], packed[half // 2 :]], axis=1)
     out_ref[: TABLE - 1, :] = packed
     out_ref[TABLE - 1 :, :] = jnp.broadcast_to(cross, (out_ref.shape[0] - TABLE + 1, LANES))
@@ -272,10 +276,22 @@
     )
     off = jnp.where(keep, both, 0.0)
     off = off + jnp.transpose(off)
-    diagonal = jnp.where(row < half, both, -jnp.sum(off, axis=1, keepdims=True))
+    diagonal = jnp.where(row < half, both, table[TABLE - 1 :, MEMBERS:])
     cross = jnp.sum(identity * table[TABLE - 1 :, :MEMBERS], axis=1, keepdims=True)
     system = jnp.where(row == lane, diagonal + (MEMBERS - 1.0), off)
-    scale = jnp.sqrt(jnp.sum(system * system, keepdims=True))
+    shape = (TABLE, LANES)
+    at = lax.broadcasted_iota(jnp.int32, shape, 0)
+    spot = lax.broadcasted_iota(jnp.int32, shape, 1)
+    body = at < TABLE - 1
+    first = spot % MEMBERS == at + half // 2 * (spot // MEMBERS)
+    second = jnp.logical_and(jnp.logical_not(body), spot >= MEMBERS + half)
+    on_diagonal = jnp.logical_or(jnp.logical_and(body, first), second)
+    squares = jnp.where(
+        on_diagonal,
+        (table + (MEMBERS - 1.0)) * (table + (MEMBERS - 1.0)),
+        jnp.where(body, 2.0 * table * table, 0.0),
+    )
+    scale = jnp.sqrt(jnp.sum(squares, keepdims=True))
     identity, system = (jnp.concatenate([x, x], axis=1) for x in (identity, system))
 
     ensemble = jnp.concatenate(

time: 91.1 us -> 91 us (level)
  no operation moved by 1% of the time
where the time goes in v4:
time: 91 us; the launch traced here: 90.6 us
  blocking collectives  76.7 us (84%)
  starting transfers between devices  7.41 us (8%)
  Pallas kernels  3.68 us (4%)
  local copies, waits for them, and re-layouts  1.55 us (2%)
  waiting for transfers between devices  1.15 us (1%)
    all_to_all x2, blocking collectives, exchange(): return lax.all_to_all(blocks, axes, split_axis=0, concat_axis=0, tiled=True)  56.1 us
    all_to_all x1, blocking collectives, per_device(): lax.all_to_all(mixed.reshape(MEMBERS, F, LANES), MEMBER, split_axis=0, co...  20.6 us
    ppermute x1, starting transfers between devices, per_device(): beside = lax.ppermute(own, SPACE, pairs + [(b, a) for a, b in pairs])  4.84 us
    pallas_call x6, Pallas kernels, call(): pl.pallas_call(body, out_shape=jax.ShapeDtypeStruct(out_shape, F32), in_s...  3.68 us
    ppermute x1, starting transfers between devices, per_device(): other = lax.ppermute(table, 'core', [(0, 1), (1, 0)])  1.92 us
  transfers between devices with their start and end apart: 3, of which 1 were waited for; matrix products, arithmetic and copies ran while one was open for 0% of the time, Pallas kernels for 1%

profile of v4, /device:TPU:6, one launch (start us, length us, event | category | flops | bytes accessed | tf_op | source)
XLA Modules:
  0.0 90.6 jit_solution(12323001838680673834)
XLA Ops:
  0.0 0.7 collective-permute-start.1
  0.7 4.8 %collective-permute-start = (f32[4,8192]{1,0:T(4,128)}, f32[4,8192]{1,0:T(4,128)S(1)}, u32[]{:S(2)}, u32[]{:S(2)}) collective-permute-start(f32[4,8192]{1,0:T(4,128)} %bitcast.20), channel_id=1, source_target_pairs={{0,1},{2,3},{4,5},{6,7},{1,0},{3,2},{5,4},{7,6},{8,9},{10,11},{12,... | collective-permute-start | bytes 393224 | tf_op jit(solution)/shard_map/ppermute | solution.py:339
  5.5 0.0 copy-start.5
  5.5 0.0 copy-start.6
  5.5 0.0 copy-start.1
  5.5 0.0 copy-start.2
  5.6 0.0 copy-start.3
  5.6 0.0 copy-start.4
  5.6 0.6 copy-done.5
  6.2 0.0 copy-done.6
  6.2 0.0 copy-done.1
  6.2 0.0 copy-done.2
  6.2 0.0 copy-done.3
  6.2 0.0 copy-done.4
  6.2 0.0 copy-start
  6.2 0.7 shard_map.73.early_ref
  6.9 0.2 copy-done
  7.2 0.2 shard_map.74.own_ref
  7.4 0.0 collective-permute-done.1.across_ref
  7.4 0.0 collective-permute-done.beside_ref
  7.4 0.4 shard_map.75
  7.8 41.0 %all_to_all.15 = f32[64,9,1,128]{3,2,1,0:T(1,128)S(1)} all-to-all(f32[64,9,1,128]{3,2,1,0:T(1,128)S(1)} %bitcast.15), channel_id=1, replica_groups=mesh['mx'=4,'mz'=8,'side'=2,'y'=4,'core'=2] {'mx','mz','side'}, dimensions={0} | all-to-all | bytes 589824 | tf_op jit(solution)/shard_map/all_to_all | solution.py:323
  48.8 0.5 shard_map.76.own_ref
  49.4 1.9 %collective-permute-start.2 = (f32[24,128]{1,0:T(8,128)S(1)}, f32[24,128]{1,0:T(8,128)S(1)}, u32[]{:S(2)}, u32[]{:S(2)}) collective-permute-start(f32[24,128]{1,0:T(8,128)S(1)} %shard_map.76.own_ref), channel_id=1, source_target_pairs={{0,1},{1,0},{2,3},{3,2},{4,5},{5,4},{6,7},{7,6},{8,9},{9,8},{10,11... | collective-permute-start | bytes 36872 | tf_op jit(solution)/shard_map/ppermute | solution.py:367
  51.3 1.1 %collective-permute-done.2.other_ref = f32[24,128]{1,0:T(8,128)S(1)} collective-permute-done((f32[24,128]{1,0:T(8,128)S(1)}, f32[24,128]{1,0:T(8,128)S(1)}, u32[]{:S(2)}, u32[]{:S(2)}) %collective-permute-start.2) | collective-permute-done | bytes 12320 | tf_op jit(solution)/shard_map/ppermute | solution.py:367
  52.5 15.1 %all_to_all.16 = f32[32,17,1,128]{3,2,1,0:T(1,128)S(1)} all-to-all(f32[32,17,1,128]{3,2,1,0:T(1,128)S(1)} %bitcast.16), channel_id=1, replica_groups=mesh['mx'=4,'mz'=8,'side'=2,'y'=4,'core'=2] {'mx','side','y'}, dimensions={0} | all-to-all | bytes 557056 | tf_op jit(solution)/shard_map/all_to_all | solution.py:323
  67.5 1.8 %shard_map.78 = f32[256,128]{1,0:T(8,128)S(1)} custom-call(f32[544,128]{1,0:T(8,128)S(1)} %bitcast.17, f32[576,128]{1,0:T(8,128)S(1)} %bitcast.14), custom_call_target="tpu_custom_call" | custom-call | tf_op jit(solution)/shard_map/pallas_call | solution.py:35
  69.3 20.6 %all_to_all.17 = f32[64,4,128]{2,1,0:T(4,128)S(1)} all-to-all(f32[64,4,128]{2,1,0:T(4,128)S(1)} %bitcast.18), channel_id=1, replica_groups=mesh['mx'=4,'mz'=8,'side'=2,'y'=4,'core'=2] {'mx','mz','side'}, dimensions={0} | all-to-all | bytes 262144 | tf_op jit(solution)/shard_map/all_to_all | solution.py:373
  89.9 0.7 copy.14
  (1 shorter events, 0.0 us)
Async XLA Ops:
  0.0 7.4 %collective-permute-start.1 = (f32[4,8192]{1,0:T(4,128)}, f32[4,8192]{1,0:T(4,128)S(1)}, u32[]{:S(2)}, u32[]{:S(2)}) collective-permute-start(f32[4,8192]{1,0:T(4,128)} %bitcast.19), channel_id=1, source_target_pairs={{1,2},{3,4},{5,6},{2,1},{4,3},{6,5},{9,10},{11,12},{13,14},{10,9},... | collective-permute-start | bytes 393224 | tf_op jit(solution)/shard_map/ppermute | solution.py:341
  0.7 6.7 %collective-permute-start = (f32[4,8192]{1,0:T(4,128)}, f32[4,8192]{1,0:T(4,128)S(1)}, u32[]{:S(2)}, u32[]{:S(2)}) collective-permute-start(f32[4,8192]{1,0:T(4,128)} %bitcast.20), channel_id=1, source_target_pairs={{0,1},{2,3},{4,5},{6,7},{1,0},{3,2},{5,4},{7,6},{8,9},{10,11},{12,... | collective-permute-start | bytes 393224 | tf_op jit(solution)/shard_map/ppermute | solution.py:339
  5.5 0.7 copy-start.5
  5.5 0.7 copy-start.6
  5.5 0.7 copy-start.1
  5.5 0.7 copy-start.2
  5.6 0.7 copy-start.3
  5.6 0.7 copy-start.4
  6.2 0.9 copy-start
  49.4 3.1 %collective-permute-start.2 = (f32[24,128]{1,0:T(8,128)S(1)}, f32[24,128]{1,0:T(8,128)S(1)}, u32[]{:S(2)}, u32[]{:S(2)}) collective-permute-start(f32[24,128]{1,0:T(8,128)S(1)} %shard_map.76.own_ref), channel_id=1, source_target_pairs={{0,1},{1,0},{2,3},{3,2},{4,5},{5,4},{6,7},{7,6},{8,9},{9,8},{10,11... | collective-permute-start | bytes 36872 | tf_op jit(solution)/shard_map/ppermute | solution.py:367

commit v5 on v4

--- a/solution.py
+++ b/solution.py
@@ -365,7 +365,7 @@
     rows = exchange(fields, MEMBER, MEMBERS).reshape(MEMBERS * MESSAGE, LANES)
     table = call(gram_body, (24, LANES), [VMEM], rows)
     other = lax.ppermute(table, "core", [(0, 1), (1, 0)])
-    group = ("mx", "side", "y")
+    group = ("y", "side", "mx")
     peers = lax.axis_size(group)
     table = call(share_body, (peers * TABLE, LANES), [VMEM, VMEM], table, other)
     table = exchange(table, group, peers).reshape(peers * TABLE, LANES)

time: 91 us -> 91.3 us (level)
  no operation moved by 1% of the time
where the time goes in v5:
time: 91.3 us; the launch traced here: 90.8 us
  blocking collectives  76.9 us (84%)
  starting transfers between devices  7.41 us (8%)
  Pallas kernels  3.68 us (4%)
  local copies, waits for them, and re-layouts  1.55 us (2%)
  waiting for transfers between devices  1.15 us (1%)
    all_to_all x2, blocking collectives, exchange(): return lax.all_to_all(blocks, axes, split_axis=0, concat_axis=0, tiled=True)  55.8 us
    all_to_all x1, blocking collectives, per_device(): lax.all_to_all(mixed.reshape(MEMBERS, F, LANES), MEMBER, split_axis=0, co...  21.1 us
    ppermute x1, starting transfers between devices, per_device(): beside = lax.ppermute(own, SPACE, pairs + [(b, a) for a, b in pairs])  4.84 us
    pallas_call x6, Pallas kernels, call(): pl.pallas_call(body, out_shape=jax.ShapeDtypeStruct(out_shape, F32), in_s...  3.68 us
    ppermute x1, starting transfers between devices, per_device(): other = lax.ppermute(table, 'core', [(0, 1), (1, 0)])  1.92 us
  transfers between devices with their start and end apart: 3, of which 1 were waited for; matrix products, arithmetic and copies ran while one was open for 0% of the time, Pallas kernels for 1%

profile of v5, /device:TPU:6, one launch (start us, length us, event | category | flops | bytes accessed | tf_op | source)
XLA Modules:
  0.0 90.8 jit_solution(14603616772786149599)
XLA Ops:
  0.0 0.7 collective-permute-start.1
  0.7 4.8 %collective-permute-start = (f32[4,8192]{1,0:T(4,128)}, f32[4,8192]{1,0:T(4,128)S(1)}, u32[]{:S(2)}, u32[]{:S(2)}) collective-permute-start(f32[4,8192]{1,0:T(4,128)} %bitcast.20), channel_id=1, source_target_pairs={{0,1},{2,3},{4,5},{6,7},{1,0},{3,2},{5,4},{7,6},{8,9},{10,11},{12,... | collective-permute-start | bytes 393224 | tf_op jit(solution)/shard_map/ppermute | solution.py:339
  5.5 0.0 copy-start.5
  5.5 0.0 copy-start.6
  5.5 0.0 copy-start.1
  5.5 0.0 copy-start.2
  5.6 0.0 copy-start.3
  5.6 0.0 copy-start.4
  5.6 0.6 copy-done.5
  6.2 0.0 copy-done.6
  6.2 0.0 copy-done.1
  6.2 0.0 copy-done.2
  6.2 0.0 copy-done.3
  6.2 0.0 copy-done.4
  6.2 0.0 copy-start
  6.2 0.7 shard_map.73.early_ref
  6.9 0.2 copy-done
  7.2 0.2 shard_map.74.own_ref
  7.4 0.0 collective-permute-done.1.across_ref
  7.4 0.0 collective-permute-done.beside_ref
  7.4 0.4 shard_map.75
  7.8 41.0 %all_to_all.15 = f32[64,9,1,128]{3,2,1,0:T(1,128)S(1)} all-to-all(f32[64,9,1,128]{3,2,1,0:T(1,128)S(1)} %bitcast.15), channel_id=1, replica_groups=mesh['mx'=4,'mz'=8,'side'=2,'y'=4,'core'=2] {'mx','mz','side'}, dimensions={0} | all-to-all | bytes 589824 | tf_op jit(solution)/shard_map/all_to_all | solution.py:323
  48.8 0.5 shard_map.76.own_ref
  49.4 1.9 %collective-permute-start.2 = (f32[24,128]{1,0:T(8,128)S(1)}, f32[24,128]{1,0:T(8,128)S(1)}, u32[]{:S(2)}, u32[]{:S(2)}) collective-permute-start(f32[24,128]{1,0:T(8,128)S(1)} %shard_map.76.own_ref), channel_id=1, source_target_pairs={{0,1},{1,0},{2,3},{3,2},{4,5},{5,4},{6,7},{7,6},{8,9},{9,8},{10,11... | collective-permute-start | bytes 36872 | tf_op jit(solution)/shard_map/ppermute | solution.py:367
  51.3 1.1 %collective-permute-done.2.other_ref = f32[24,128]{1,0:T(8,128)S(1)} collective-permute-done((f32[24,128]{1,0:T(8,128)S(1)}, f32[24,128]{1,0:T(8,128)S(1)}, u32[]{:S(2)}, u32[]{:S(2)}) %collective-permute-start.2) | collective-permute-done | bytes 12320 | tf_op jit(solution)/shard_map/ppermute | solution.py:367
  52.5 14.8 %all_to_all.16 = f32[32,17,1,128]{3,2,1,0:T(1,128)S(1)} all-to-all(f32[32,17,1,128]{3,2,1,0:T(1,128)S(1)} %bitcast.16), channel_id=1, replica_groups=mesh['mx'=4,'mz'=8,'side'=2,'y'=4,'core'=2] {'y','side','mx'}, dimensions={0} | all-to-all | bytes 557056 | tf_op jit(solution)/shard_map/all_to_all | solution.py:323
  67.2 1.8 %shard_map.78 = f32[256,128]{1,0:T(8,128)S(1)} custom-call(f32[544,128]{1,0:T(8,128)S(1)} %bitcast.17, f32[576,128]{1,0:T(8,128)S(1)} %bitcast.14), custom_call_target="tpu_custom_call" | custom-call | tf_op jit(solution)/shard_map/pallas_call | solution.py:35
  69.0 21.1 %all_to_all.17 = f32[64,4,128]{2,1,0:T(4,128)S(1)} all-to-all(f32[64,4,128]{2,1,0:T(4,128)S(1)} %bitcast.18), channel_id=1, replica_groups=mesh['mx'=4,'mz'=8,'side'=2,'y'=4,'core'=2] {'mx','mz','side'}, dimensions={0} | all-to-all | bytes 262144 | tf_op jit(solution)/shard_map/all_to_all | solution.py:373
  90.2 0.7 copy.14
  (1 shorter events, 0.0 us)
Async XLA Ops:
  0.0 7.4 %collective-permute-start.1 = (f32[4,8192]{1,0:T(4,128)}, f32[4,8192]{1,0:T(4,128)S(1)}, u32[]{:S(2)}, u32[]{:S(2)}) collective-permute-start(f32[4,8192]{1,0:T(4,128)} %bitcast.19), channel_id=1, source_target_pairs={{1,2},{3,4},{5,6},{2,1},{4,3},{6,5},{9,10},{11,12},{13,14},{10,9},... | collective-permute-start | bytes 393224 | tf_op jit(solution)/shard_map/ppermute | solution.py:341
  0.7 6.7 %collective-permute-start = (f32[4,8192]{1,0:T(4,128)}, f32[4,8192]{1,0:T(4,128)S(1)}, u32[]{:S(2)}, u32[]{:S(2)}) collective-permute-start(f32[4,8192]{1,0:T(4,128)} %bitcast.20), channel_id=1, source_target_pairs={{0,1},{2,3},{4,5},{6,7},{1,0},{3,2},{5,4},{7,6},{8,9},{10,11},{12,... | collective-permute-start | bytes 393224 | tf_op jit(solution)/shard_map/ppermute | solution.py:339
  5.5 0.7 copy-start.5
  5.5 0.7 copy-start.6
  5.5 0.7 copy-start.1
  5.5 0.7 copy-start.2
  5.6 0.7 copy-start.3
  5.6 0.7 copy-start.4
  6.2 0.9 copy-start
  49.4 3.1 %collective-permute-start.2 = (f32[24,128]{1,0:T(8,128)S(1)}, f32[24,128]{1,0:T(8,128)S(1)}, u32[]{:S(2)}, u32[]{:S(2)}) collective-permute-start(f32[24,128]{1,0:T(8,128)S(1)} %shard_map.76.own_ref), channel_id=1, source_target_pairs={{0,1},{1,0},{2,3},{3,2},{4,5},{5,4},{6,7},{7,6},{8,9},{9,8},{10,11... | collective-permute-start | bytes 36872 | tf_op jit(solution)/shard_map/ppermute | solution.py:367

commit v6 on v4

--- a/solution.py
+++ b/solution.py
@@ -25,7 +25,6 @@
 TABLE = MEMBERS * MEMBERS // 2 // LANES + 1
 
 VMEM = pl.BlockSpec(memory_space=pltpu.VMEM)
-SMEM = pl.BlockSpec(memory_space=pltpu.SMEM)
 F32 = jnp.float32
 MEMBER = ("mx", "mz", "side")
 SPACE = ("y", "core")
@@ -84,25 +83,32 @@
     return jnp.sum(share, axis=0, keepdims=True)
 
 
-def early_body(diffusion_ref, velocity_ref, position_ref, choice_ref, value_ref, var_ref, out_ref):
+def mask_body(out_ref):
+    inner_z = lax.broadcasted_iota(jnp.int32, (8, LANES), 1) % NZ
+    out_ref[:8, :] = jnp.where(inner_z != NZ - 1, 1.0, 0.0)
+    out_ref[8:, :] = jnp.where(inner_z != 0, 1.0, 0.0)
+
+
+def early_body(
+    mask_ref, diffusion_ref, velocity_ref, position_ref, choice_ref, value_ref, var_ref, out_ref
+):
     shape = (2 * F, LANES)
     field = lax.broadcasted_iota(jnp.int32, shape, 0) % F
-    inner_z = lax.broadcasted_iota(jnp.int32, shape, 1) % NZ
-
-    def per_field(values):
-        tile = jnp.full(shape, values[F - 1], F32)
+
+    def per_field(row):
+        tile = jnp.broadcast_to(row[:, F - 1 :], shape)
         for f in range(F - 1):
-            tile = jnp.where(field == f, values[f], tile)
+            tile = jnp.where(field == f, jnp.broadcast_to(row[:, f : f + 1], shape), tile)
         return tile
 
-    diffuse = per_field([diffusion_ref[f] for f in range(F)])
-    move = [per_field([0.5 * velocity_ref[a, f] for f in range(F)]) for a in range(3)]
+    diffuse = per_field(diffusion_ref[...])
+    move = [per_field(0.5 * velocity_ref[a : a + 1, :]) for a in range(3)]
     coef = (
         1.0 - 6.0 * diffuse,
         diffuse - move[1],
         diffuse + move[1],
-        jnp.where(inner_z != NZ - 1, diffuse - move[2], 0.0),
-        jnp.where(inner_z != 0, diffuse + move[2], 0.0),
+        (diffuse - move[2]) * mask_ref[:8, :],
+        (diffuse + move[2]) * mask_ref[8:, :],
         diffuse - move[0],
         diffuse + move[0],
     )
@@ -339,17 +345,19 @@
     beside = lax.ppermute(own, SPACE, pairs + [(b, a) for a, b in pairs])
     pairs = [(i, i + 1) for i in range(1, slabs - 1, 2)]
     across = lax.ppermute(own, SPACE, pairs + [(b, a) for a, b in pairs])
+    mask = call(mask_body, (16, LANES), [], flops=100 * FLOPS)
     early = call(
         early_body,
         (SUMS + 8, LANES),
-        [SMEM, SMEM] + [VMEM] * 4,
-        diffusion,
+        [VMEM] * 7,
+        mask,
+        diffusion.reshape(1, -1),
         velocity,
         detector_voxel_position.reshape(1, -1),
         detector_quantity_choice.reshape(1, -1),
         sensor_value.reshape(1, -1),
         sensor_var.reshape(1, -1),
-        flops=FLOPS,
+        flops=1,
     )
     planes = call(own_body, (2 * FLAT, LANES), [VMEM] * 2, early, own, flops=FLOPS)
     fields = call(

time: 91 us -> 90.8 us (level)
    pallas_call x6 -> x7, Pallas kernels: 3.68 us -> 3.12 us  [call(): pl.pallas_call(body, out_shape=jax.ShapeDtypeStruct(out_shape, F32), in_s...]
  transfers between devices with their start and end apart: 3 -> 3, of which waited for: 1 -> 2; matrix products, arithmetic and copies ran while one was open for 0% -> 0% of each run, Pallas kernels for 1% -> 0%
where the time goes in v6:
time: 90.8 us; the launch traced here: 90.4 us
  blocking collectives  77.1 us (85%)
  starting transfers between devices  7.54 us (8%)
  Pallas kernels  3.12 us (3%)
  local copies, waits for them, and re-layouts  1.33 us (1%)
  waiting for transfers between devices  1.22 us (1%)
    all_to_all x2, blocking collectives, exchange(): return lax.all_to_all(blocks, axes, split_axis=0, concat_axis=0, tiled=True)  56.3 us
    all_to_all x1, blocking collectives, per_device(): lax.all_to_all(mixed.reshape(MEMBERS, F, LANES), MEMBER, split_axis=0, co...  20.8 us
    ppermute x1, starting transfers between devices, per_device(): beside = lax.ppermute(own, SPACE, pairs + [(b, a) for a, b in pairs])  4.84 us
    pallas_call x7, Pallas kernels, call(): pl.pallas_call(body, out_shape=jax.ShapeDtypeStruct(out_shape, F32), in_s...  3.12 us
    ppermute x1, starting transfers between devices, per_device(): other = lax.ppermute(table, 'core', [(0, 1), (1, 0)])  1.92 us
  transfers between devices with their start and end apart: 3, of which 2 were waited for; matrix products, arithmetic and copies ran while one was open for 0% of the time, Pallas kernels for 0%

profile of v6, /device:TPU:6, one launch (start us, length us, event | category | flops | bytes accessed | tf_op | source)
XLA Modules:
  0.0 90.4 jit_solution(10139841752381871131)
XLA Ops:
  0.0 0.0 copy-start
  0.0 0.8 collective-permute-start.1
  0.8 4.8 %collective-permute-start = (f32[4,8192]{1,0:T(4,128)}, f32[4,8192]{1,0:T(4,128)S(1)}, u32[]{:S(2)}, u32[]{:S(2)}) collective-permute-start(f32[4,8192]{1,0:T(4,128)} %bitcast.21), channel_id=1, source_target_pairs={{0,1},{2,3},{4,5},{6,7},{1,0},{3,2},{5,4},{7,6},{8,9},{10,11},{12,... | collective-permute-start | bytes 393224 | tf_op jit(solution)/shard_map/ppermute | solution.py:345
  5.6 0.0 copy-start.5
  5.7 0.0 copy-start.6
  5.7 0.0 copy-start.1
  5.7 0.0 copy-start.2
  5.7 0.0 copy-start.3
  5.7 0.0 copy-start.4
  5.7 0.6 copy-done.5
  6.3 0.0 copy-done.6
  6.3 0.0 copy-done.1
  6.4 0.0 copy-done.2
  6.4 0.0 copy-done.3
  6.4 0.0 copy-done.4
  6.4 0.1 shard_map.74.early_ref
  6.5 0.0 copy-done
  6.5 0.2 shard_map.75.own_ref
  6.7 0.0 collective-permute-done.1.across_ref
  6.7 0.1 collective-permute-done.beside_ref
  6.8 0.4 shard_map.76
  7.3 41.4 %all_to_all.15 = f32[64,9,1,128]{3,2,1,0:T(1,128)S(1)} all-to-all(f32[64,9,1,128]{3,2,1,0:T(1,128)S(1)} %bitcast.16), channel_id=1, replica_groups=mesh['mx'=4,'mz'=8,'side'=2,'y'=4,'core'=2] {'mx','mz','side'}, dimensions={0} | all-to-all | bytes 589824 | tf_op jit(solution)/shard_map/all_to_all | solution.py:329
  48.6 0.5 shard_map.77.own_ref
  49.2 1.9 %collective-permute-start.2 = (f32[24,128]{1,0:T(8,128)S(1)}, f32[24,128]{1,0:T(8,128)S(1)}, u32[]{:S(2)}, u32[]{:S(2)}) collective-permute-start(f32[24,128]{1,0:T(8,128)S(1)} %shard_map.77.own_ref), channel_id=1, source_target_pairs={{0,1},{1,0},{2,3},{3,2},{4,5},{5,4},{6,7},{7,6},{8,9},{9,8},{10,11... | collective-permute-start | bytes 36872 | tf_op jit(solution)/shard_map/ppermute | solution.py:375
  51.1 1.1 %collective-permute-done.2.other_ref = f32[24,128]{1,0:T(8,128)S(1)} collective-permute-done((f32[24,128]{1,0:T(8,128)S(1)}, f32[24,128]{1,0:T(8,128)S(1)}, u32[]{:S(2)}, u32[]{:S(2)}) %collective-permute-start.2) | collective-permute-done | bytes 12320 | tf_op jit(solution)/shard_map/ppermute | solution.py:375
  52.3 14.9 %all_to_all.16 = f32[32,17,1,128]{3,2,1,0:T(1,128)S(1)} all-to-all(f32[32,17,1,128]{3,2,1,0:T(1,128)S(1)} %bitcast.17), channel_id=1, replica_groups=mesh['mx'=4,'mz'=8,'side'=2,'y'=4,'core'=2] {'mx','side','y'}, dimensions={0} | all-to-all | bytes 557056 | tf_op jit(solution)/shard_map/all_to_all | solution.py:329
  67.2 1.8 %shard_map.79 = f32[256,128]{1,0:T(8,128)S(1)} custom-call(f32[544,128]{1,0:T(8,128)S(1)} %bitcast.18, f32[576,128]{1,0:T(8,128)S(1)} %bitcast.15), custom_call_target="tpu_custom_call" | custom-call | tf_op jit(solution)/shard_map/pallas_call | solution.py:34
  69.0 20.8 %all_to_all.17 = f32[64,4,128]{2,1,0:T(4,128)S(1)} all-to-all(f32[64,4,128]{2,1,0:T(4,128)S(1)} %bitcast.19), channel_id=1, replica_groups=mesh['mx'=4,'mz'=8,'side'=2,'y'=4,'core'=2] {'mx','mz','side'}, dimensions={0} | all-to-all | bytes 262144 | tf_op jit(solution)/shard_map/all_to_all | solution.py:381
  89.8 0.7 copy.14
  (2 shorter events, 0.0 us)
Async XLA Ops:
  0.0 6.5 %copy-start = (f32[1,4,8192]{2,1,0:T(4,128)S(1)}, f32[1,4,8192]{2,1,0:T(4,128)}, u32[]{:S(2)}) copy-start(f32[1,4,8192]{2,1,0:T(4,128)} %param.7) | copy-start | bytes 393220
  0.0 6.7 %collective-permute-start.1 = (f32[4,8192]{1,0:T(4,128)}, f32[4,8192]{1,0:T(4,128)S(1)}, u32[]{:S(2)}, u32[]{:S(2)}) collective-permute-start(f32[4,8192]{1,0:T(4,128)} %bitcast.20), channel_id=1, source_target_pairs={{1,2},{3,4},{5,6},{2,1},{4,3},{6,5},{9,10},{11,12},{13,14},{10,9},... | collective-permute-start | bytes 393224 | tf_op jit(solution)/shard_map/ppermute | solution.py:347
  0.8 6.0 %collective-permute-start = (f32[4,8192]{1,0:T(4,128)}, f32[4,8192]{1,0:T(4,128)S(1)}, u32[]{:S(2)}, u32[]{:S(2)}) collective-permute-start(f32[4,8192]{1,0:T(4,128)} %bitcast.21), channel_id=1, source_target_pairs={{0,1},{2,3},{4,5},{6,7},{1,0},{3,2},{5,4},{7,6},{8,9},{10,11},{12,... | collective-permute-start | bytes 393224 | tf_op jit(solution)/shard_map/ppermute | solution.py:345
  5.6 0.7 copy-start.5
  5.7 0.7 copy-start.6
  5.7 0.7 copy-start.1
  5.7 0.7 copy-start.2
  5.7 0.7 copy-start.3
  5.7 0.7 copy-start.4
  49.2 3.1 %collective-permute-start.2 = (f32[24,128]{1,0:T(8,128)S(1)}, f32[24,128]{1,0:T(8,128)S(1)}, u32[]{:S(2)}, u32[]{:S(2)}) collective-permute-start(f32[24,128]{1,0:T(8,128)S(1)} %shard_map.77.own_ref), channel_id=1, source_target_pairs={{0,1},{1,0},{2,3},{3,2},{4,5},{5,4},{6,7},{7,6},{8,9},{9,8},{10,11... | collective-permute-start | bytes 36872 | tf_op jit(solution)/shard_map/ppermute | solution.py:375

commit v7 on v6

--- a/solution.py
+++ b/solution.py
@@ -308,7 +308,8 @@
         [ensemble - centre, jnp.broadcast_to(cross, (MEMBERS, LANES))], axis=1
     )
 
-    root = system / scale
+    inverse_scale = 1.0 / scale
+    root = system * inverse_scale
     inverse_root = 1.5 * identity - 0.5 * root
     root = mm(root, inverse_root)
     for step in range(1, NS_ITERS):
@@ -317,11 +318,13 @@
             both = mm(jnp.concatenate([root, inverse_root], axis=0), factor)
             root, inverse_root = both[:MEMBERS], both[MEMBERS:]
     wide = mm(factor, mm(inverse_root, wide))
-    anomaly, drive = wide[:, : F * LANES], wide[:, F * LANES : F * LANES + 1] / scale
-    shift = jnp.sum(drive * anomaly, axis=0, keepdims=True)
-    mixed = (centre + shift) + anomaly * (math.sqrt(MEMBERS - 1.0) / jnp.sqrt(scale))
+    drive = wide[:, F * LANES :]
+    gain = math.sqrt(MEMBERS - 1.0) / jnp.sqrt(scale)
     for f in range(F):
-        out_ref[pl.ds(f, MEMBERS, stride=F), :] = mixed[:, f * LANES : (f + 1) * LANES]
+        lanes = slice(f * LANES, (f + 1) * LANES)
+        anomaly = wide[:, lanes]
+        shift = jnp.sum(drive * anomaly, axis=0, keepdims=True) * inverse_scale
+        out_ref[pl.ds(f, MEMBERS, stride=F), :] = (centre[:, lanes] + shift) + anomaly * gain
 
 
 def exchange(rows, axes, peers):

time: 90.8 us -> 90.8 us (level)
  no operation moved by 1% of the time
where the time goes in v7:
time: 90.8 us; the launch traced here: 90.3 us
  blocking collectives  77.1 us (85%)
  starting transfers between devices  7.54 us (8%)
  Pallas kernels  3.05 us (3%)
  local copies, waits for them, and re-layouts  1.33 us (1%)
  waiting for transfers between devices  1.22 us (1%)
    all_to_all x2, blocking collectives, exchange(): return lax.all_to_all(blocks, axes, split_axis=0, concat_axis=0, tiled=True)  56.3 us
    all_to_all x1, blocking collectives, per_device(): lax.all_to_all(mixed.reshape(MEMBERS, F, LANES), MEMBER, split_axis=0, co...  20.8 us
    ppermute x1, starting transfers between devices, per_device(): beside = lax.ppermute(own, SPACE, pairs + [(b, a) for a, b in pairs])  4.84 us
    pallas_call x7, Pallas kernels, call(): pl.pallas_call(body, out_shape=jax.ShapeDtypeStruct(out_shape, F32), in_s...  3.05 us
    ppermute x1, starting transfers between devices, per_device(): other = lax.ppermute(table, 'core', [(0, 1), (1, 0)])  1.92 us
  transfers between devices with their start and end apart: 3, of which 2 were waited for; matrix products, arithmetic and copies ran while one was open for 0% of the time, Pallas kernels for 0%

profile of v7, /device:TPU:6, one launch (start us, length us, event | category | flops | bytes accessed | tf_op | source)
XLA Modules:
  0.0 90.3 jit_solution(227692110114067807)
XLA Ops:
  0.0 0.0 copy-start
  0.0 0.8 collective-permute-start.1
  0.8 4.8 %collective-permute-start = (f32[4,8192]{1,0:T(4,128)}, f32[4,8192]{1,0:T(4,128)S(1)}, u32[]{:S(2)}, u32[]{:S(2)}) collective-permute-start(f32[4,8192]{1,0:T(4,128)} %bitcast.21), channel_id=1, source_target_pairs={{0,1},{2,3},{4,5},{6,7},{1,0},{3,2},{5,4},{7,6},{8,9},{10,11},{12,... | collective-permute-start | bytes 393224 | tf_op jit(solution)/shard_map/ppermute | solution.py:348
  5.6 0.0 copy-start.5
  5.7 0.0 copy-start.6
  5.7 0.0 copy-start.1
  5.7 0.0 copy-start.2
  5.7 0.0 copy-start.3
  5.7 0.0 copy-start.4
  5.7 0.6 copy-done.5
  6.3 0.0 copy-done.6
  6.3 0.0 copy-done.1
  6.4 0.0 copy-done.2
  6.4 0.0 copy-done.3
  6.4 0.0 copy-done.4
  6.4 0.1 shard_map.74.early_ref
  6.5 0.0 copy-done
  6.5 0.2 shard_map.75.own_ref
  6.7 0.0 collective-permute-done.1.across_ref
  6.7 0.1 collective-permute-done.beside_ref
  6.8 0.4 shard_map.76
  7.3 41.4 %all_to_all.15 = f32[64,9,1,128]{3,2,1,0:T(1,128)S(1)} all-to-all(f32[64,9,1,128]{3,2,1,0:T(1,128)S(1)} %bitcast.16), channel_id=1, replica_groups=mesh['mx'=4,'mz'=8,'side'=2,'y'=4,'core'=2] {'mx','mz','side'}, dimensions={0} | all-to-all | bytes 589824 | tf_op jit(solution)/shard_map/all_to_all | solution.py:332
  48.6 0.5 shard_map.77.own_ref
  49.2 1.9 %collective-permute-start.2 = (f32[24,128]{1,0:T(8,128)S(1)}, f32[24,128]{1,0:T(8,128)S(1)}, u32[]{:S(2)}, u32[]{:S(2)}) collective-permute-start(f32[24,128]{1,0:T(8,128)S(1)} %shard_map.77.own_ref), channel_id=1, source_target_pairs={{0,1},{1,0},{2,3},{3,2},{4,5},{5,4},{6,7},{7,6},{8,9},{9,8},{10,11... | collective-permute-start | bytes 36872 | tf_op jit(solution)/shard_map/ppermute | solution.py:378
  51.1 1.1 %collective-permute-done.2.other_ref = f32[24,128]{1,0:T(8,128)S(1)} collective-permute-done((f32[24,128]{1,0:T(8,128)S(1)}, f32[24,128]{1,0:T(8,128)S(1)}, u32[]{:S(2)}, u32[]{:S(2)}) %collective-permute-start.2) | collective-permute-done | bytes 12320 | tf_op jit(solution)/shard_map/ppermute | solution.py:378
  52.3 14.9 %all_to_all.16 = f32[32,17,1,128]{3,2,1,0:T(1,128)S(1)} all-to-all(f32[32,17,1,128]{3,2,1,0:T(1,128)S(1)} %bitcast.17), channel_id=1, replica_groups=mesh['mx'=4,'mz'=8,'side'=2,'y'=4,'core'=2] {'mx','side','y'}, dimensions={0} | all-to-all | bytes 557056 | tf_op jit(solution)/shard_map/all_to_all | solution.py:332
  67.2 1.7 %shard_map.79 = f32[256,128]{1,0:T(8,128)S(1)} custom-call(f32[544,128]{1,0:T(8,128)S(1)} %bitcast.18, f32[576,128]{1,0:T(8,128)S(1)} %bitcast.15), custom_call_target="tpu_custom_call" | custom-call | tf_op jit(solution)/shard_map/pallas_call | solution.py:34
  68.9 20.8 %all_to_all.17 = f32[64,4,128]{2,1,0:T(4,128)S(1)} all-to-all(f32[64,4,128]{2,1,0:T(4,128)S(1)} %bitcast.19), channel_id=1, replica_groups=mesh['mx'=4,'mz'=8,'side'=2,'y'=4,'core'=2] {'mx','mz','side'}, dimensions={0} | all-to-all | bytes 262144 | tf_op jit(solution)/shard_map/all_to_all | solution.py:384
  89.7 0.7 copy.14
  (2 shorter events, 0.0 us)
Async XLA Ops:
  0.0 6.5 %copy-start = (f32[1,4,8192]{2,1,0:T(4,128)S(1)}, f32[1,4,8192]{2,1,0:T(4,128)}, u32[]{:S(2)}) copy-start(f32[1,4,8192]{2,1,0:T(4,128)} %param.7) | copy-start | bytes 393220
  0.0 6.7 %collective-permute-start.1 = (f32[4,8192]{1,0:T(4,128)}, f32[4,8192]{1,0:T(4,128)S(1)}, u32[]{:S(2)}, u32[]{:S(2)}) collective-permute-start(f32[4,8192]{1,0:T(4,128)} %bitcast.20), channel_id=1, source_target_pairs={{1,2},{3,4},{5,6},{2,1},{4,3},{6,5},{9,10},{11,12},{13,14},{10,9},... | collective-permute-start | bytes 393224 | tf_op jit(solution)/shard_map/ppermute | solution.py:350
  0.8 6.0 %collective-permute-start = (f32[4,8192]{1,0:T(4,128)}, f32[4,8192]{1,0:T(4,128)S(1)}, u32[]{:S(2)}, u32[]{:S(2)}) collective-permute-start(f32[4,8192]{1,0:T(4,128)} %bitcast.21), channel_id=1, source_target_pairs={{0,1},{2,3},{4,5},{6,7},{1,0},{3,2},{5,4},{7,6},{8,9},{10,11},{12,... | collective-permute-start | bytes 393224 | tf_op jit(solution)/shard_map/ppermute | solution.py:348
  5.6 0.7 copy-start.5
  5.7 0.7 copy-start.6
  5.7 0.7 copy-start.1
  5.7 0.7 copy-start.2
  5.7 0.7 copy-start.3
  5.7 0.7 copy-start.4
  49.2 3.1 %collective-permute-start.2 = (f32[24,128]{1,0:T(8,128)S(1)}, f32[24,128]{1,0:T(8,128)S(1)}, u32[]{:S(2)}, u32[]{:S(2)}) collective-permute-start(f32[24,128]{1,0:T(8,128)S(1)} %shard_map.77.own_ref), channel_id=1, source_target_pairs={{0,1},{1,0},{2,3},{3,2},{4,5},{5,4},{6,7},{7,6},{8,9},{9,8},{10,11... | collective-permute-start | bytes 36872 | tf_op jit(solution)/shard_map/ppermute | solution.py:378

commit v8 on v7

--- a/solution.py
+++ b/solution.py
@@ -19,7 +19,7 @@
 PLANE = NY * NZ
 CHUNKS = PLANE // LANES
 FLAT = 8 * CHUNKS
-SUMS = 8 * 7
+SUMS = 8 * 10
 FLOPS = 10**8
 MESSAGE = 2 * F + 1
 TABLE = MEMBERS * MEMBERS // 2 // LANES + 1
@@ -111,6 +111,9 @@
         (diffuse + move[2]) * mask_ref[8:, :],
         diffuse - move[0],
         diffuse + move[0],
+        diffuse,
+        move[1],
+        move[2],
     )
     for i in range(len(coef)):
         out_ref[8 * i : 8 * i + 8, :] = coef[i]
@@ -120,12 +123,22 @@
     )
 
 
-def own_body(early_ref, own_ref, out_ref):
+def own_body(mask_ref, own_ref, out_ref):
     own = [stack(own_ref[:, tile(0, j)], own_ref[:, tile(1, j)]) for j in range(CHUNKS)]
-    flat = in_plane(own, [early_ref[8 * i : 8 * i + 8, :] for i in range(5)])
+    lane = lax.broadcasted_iota(jnp.int32, (8, LANES), 1)
+    up = [pltpu.roll(x, LANES - NZ, 1) for x in own]
+    down = [pltpu.roll(x, NZ, 1) for x in own]
+    zero = jnp.zeros_like(own[0])
     for j in range(CHUNKS):
-        out_ref[8 * j : 8 * j + 8, :] = own[j]
-        out_ref[FLAT + 8 * j : FLAT + 8 * j + 8, :] = flat[j]
+        after = up[j + 1] if j + 1 < CHUNKS else zero
+        before = down[j - 1] if j > 0 else zero
+        y_next = jnp.where(lane < LANES - NZ, up[j], after)
+        y_prev = jnp.where(lane >= NZ, down[j], before)
+        z_next = pltpu.roll(own[j], LANES - 1, 1) * mask_ref[:8, :]
+        z_prev = pltpu.roll(own[j], 1, 1) * mask_ref[8:, :]
+        parts = (own[j], y_next + y_prev + (z_next + z_prev), y_next - y_prev, z_next - z_prev)
+        for i in range(4):
+            out_ref[i * FLAT + 8 * j : i * FLAT + 8 * j + 8, :] = parts[i]
 
 
 def tile(plane, chunk):
@@ -135,8 +148,8 @@
 def forecast_body(early_ref, own_ref, beside_ref, across_ref, out_ref):
     slab = lax.axis_index(SPACE)
     even = slab % 2 == 0
-    coef = [early_ref[8 * i : 8 * i + 8, :] for i in range(7)]
-    x_next, x_prev = coef[5:]
+    coef = [early_ref[8 * i : 8 * i + 8, :] for i in range(10)]
+    x_next, x_prev, spread, y_move, z_move = coef[5:]
     own = [own_ref[8 * j : 8 * j + 8, :] for j in range(CHUNKS)]
 
     def neighbour(first_ref, second_ref, plane, j):
@@ -162,7 +175,10 @@
         for j in range(CHUNKS)
     ]
     inner = [
-        own_ref[FLAT + 8 * j : FLAT + 8 * j + 8, :]
+        coef[0] * own[j]
+        + spread * own_ref[FLAT + 8 * j : FLAT + 8 * j + 8, :]
+        - y_move * own_ref[2 * FLAT + 8 * j : 2 * FLAT + 8 * j + 8, :]
+        - z_move * own_ref[3 * FLAT + 8 * j : 3 * FLAT + 8 * j + 8, :]
         + x_next * stack(own[j][F:], halo[j][F:])
         + x_prev * stack(halo[j][:F], own[j][:F])
         for j in range(CHUNKS)
@@ -349,6 +365,7 @@
     pairs = [(i, i + 1) for i in range(1, slabs - 1, 2)]
     across = lax.ppermute(own, SPACE, pairs + [(b, a) for a, b in pairs])
     mask = call(mask_body, (16, LANES), [], flops=100 * FLOPS)
+    planes = call(own_body, (4 * FLAT, LANES), [VMEM] * 2, mask, own, flops=10**14)
     early = call(
         early_body,
         (SUMS + 8, LANES),
@@ -362,7 +379,6 @@
         sensor_var.reshape(1, -1),
         flops=1,
     )
-    planes = call(own_body, (2 * FLAT, LANES), [VMEM] * 2, early, own, flops=FLOPS)
     fields = call(
         forecast_body,
         (MEMBERS * MESSAGE, LANES),

time: 90.8 us -> 91.9 us (1.012)
  Pallas kernels: 3.05 us -> 4.03 us
    pallas_call x7, Pallas kernels: 3.05 us -> 4.03 us  [call(): pl.pallas_call(body, out_shape=jax.ShapeDtypeStruct(out_shape, F32), in_s...]
where the time goes in v8:
time: 91.9 us; the launch traced here: 91.4 us
  blocking collectives  77 us (84%)
  starting transfers between devices  7.55 us (8%)
  Pallas kernels  4.03 us (4%)
  waiting for transfers between devices  1.54 us (2%)
  local copies, waits for them, and re-layouts  1.14 us (1%)
    all_to_all x2, blocking collectives, exchange(): return lax.all_to_all(blocks, axes, split_axis=0, concat_axis=0, tiled=True)  56.4 us
    all_to_all x1, blocking collectives, per_device(): lax.all_to_all(mixed.reshape(MEMBERS, F, LANES), MEMBER, split_axis=0, co...  20.6 us
    ppermute x1, starting transfers between devices, per_device(): beside = lax.ppermute(own, SPACE, pairs + [(b, a) for a, b in pairs])  4.2 us
    pallas_call x7, Pallas kernels, call(): pl.pallas_call(body, out_shape=jax.ShapeDtypeStruct(out_shape, F32), in_s...  4.03 us
    ppermute x1, starting transfers between devices, per_device(): other = lax.ppermute(table, 'core', [(0, 1), (1, 0)])  1.92 us
  transfers between devices with their start and end apart: 3, of which 2 were waited for; matrix products, arithmetic and copies ran while one was open for 0% of the time, Pallas kernels for 0%

profile of v8, /device:TPU:6, one launch (start us, length us, event | category | flops | bytes accessed | tf_op | source)
XLA Modules:
  0.0 91.4 jit_solution(18418799463247035082)
XLA Ops:
  0.0 0.0 copy-start.6
  0.0 1.4 %collective-permute-start.1 = (f32[4,8192]{1,0:T(4,128)}, f32[4,8192]{1,0:T(4,128)}, u32[]{:S(2)}, u32[]{:S(2)}) collective-permute-start(f32[4,8192]{1,0:T(4,128)} %bitcast.25), channel_id=1, source_target_pairs={{1,2},{3,4},{5,6},{2,1},{4,3},{6,5},{9,10},{11,12},{13,14},{10,9},... | collective-permute-start | bytes 393224 | tf_op jit(solution)/shard_map/ppermute | solution.py:366
  1.4 4.2 %collective-permute-start = (f32[4,8192]{1,0:T(4,128)}, f32[4,8192]{1,0:T(4,128)}, u32[]{:S(2)}, u32[]{:S(2)}) collective-permute-start(f32[4,8192]{1,0:T(4,128)} %bitcast.26), channel_id=1, source_target_pairs={{0,1},{2,3},{4,5},{6,7},{1,0},{3,2},{5,4},{7,6},{8,9},{10,11},{12,... | collective-permute-start | bytes 393224 | tf_op jit(solution)/shard_map/ppermute | solution.py:364
  5.7 0.0 copy-done.6
  5.7 0.0 copy-start
  5.7 0.0 copy-start.1
  5.7 0.0 copy-start.2
  5.7 0.0 copy-start.3
  5.7 0.0 copy-start.4
  5.7 0.0 copy-start.5
  5.7 0.2 shard_map.75.own_ref
  6.0 0.4 copy-done
  6.4 0.0 copy-done.1
  6.4 0.0 copy-done.2
  6.4 0.0 copy-done.3
  6.4 0.0 copy-done.4
  6.4 0.0 copy-done.5
  6.4 0.1 shard_map.74.early_ref
  6.5 0.0 collective-permute-done.1.across_ref
  6.6 0.4 collective-permute-done.beside_ref
  7.0 1.4 %shard_map.76 = f32[576,128]{1,0:T(8,128)S(1)} custom-call(f32[88,128]{1,0:T(8,128)S(1)} %shard_map.74.early_ref, f32[1024,128]{1,0:T(8,128)S(1)} %shard_map.75.own_ref, f32[4,8192]{1,0:T(4,128)} %collective-permute-done.beside_ref, f32[4,8192]{1,0:T(4,128)} %collective-permute-done.1.across_ref), custom_call_target="tpu_custom_call" | custom-call | flops 100000000 | bytes 262144 | tf_op jit(solution)/shard_map/pallas_call | solution.py:34
  8.4 41.4 %all_to_all.15 = f32[64,9,1,128]{3,2,1,0:T(1,128)S(1)} all-to-all(f32[64,9,1,128]{3,2,1,0:T(1,128)S(1)} %bitcast.16), channel_id=1, replica_groups=mesh['mx'=4,'mz'=8,'side'=2,'y'=4,'core'=2] {'mx','mz','side'}, dimensions={0} | all-to-all | bytes 589824 | tf_op jit(solution)/shard_map/all_to_all | solution.py:348
  49.7 0.5 shard_map.77.own_ref
  50.3 1.9 %collective-permute-start.2 = (f32[24,128]{1,0:T(8,128)S(1)}, f32[24,128]{1,0:T(8,128)S(1)}, u32[]{:S(2)}, u32[]{:S(2)}) collective-permute-start(f32[24,128]{1,0:T(8,128)S(1)} %shard_map.77.own_ref), channel_id=1, source_target_pairs={{0,1},{1,0},{2,3},{3,2},{4,5},{5,4},{6,7},{7,6},{8,9},{9,8},{10,11... | collective-permute-start | bytes 36872 | tf_op jit(solution)/shard_map/ppermute | solution.py:394
  52.2 1.1 %collective-permute-done.2.other_ref = f32[24,128]{1,0:T(8,128)S(1)} collective-permute-done((f32[24,128]{1,0:T(8,128)S(1)}, f32[24,128]{1,0:T(8,128)S(1)}, u32[]{:S(2)}, u32[]{:S(2)}) %collective-permute-start.2) | collective-permute-done | bytes 12320 | tf_op jit(solution)/shard_map/ppermute | solution.py:394
  53.4 15.0 %all_to_all.16 = f32[32,17,1,128]{3,2,1,0:T(1,128)S(1)} all-to-all(f32[32,17,1,128]{3,2,1,0:T(1,128)S(1)} %bitcast.17), channel_id=1, replica_groups=mesh['mx'=4,'mz'=8,'side'=2,'y'=4,'core'=2] {'mx','side','y'}, dimensions={0} | all-to-all | bytes 557056 | tf_op jit(solution)/shard_map/all_to_all | solution.py:348
  68.4 1.7 %shard_map.79 = f32[256,128]{1,0:T(8,128)S(1)} custom-call(f32[544,128]{1,0:T(8,128)S(1)} %bitcast.18, f32[576,128]{1,0:T(8,128)S(1)} %bitcast.15), custom_call_target="tpu_custom_call" | custom-call | tf_op jit(solution)/shard_map/pallas_call | solution.py:34
  70.1 20.6 %all_to_all.17 = f32[64,4,128]{2,1,0:T(4,128)S(1)} all-to-all(f32[64,4,128]{2,1,0:T(4,128)S(1)} %bitcast.19), channel_id=1, replica_groups=mesh['mx'=4,'mz'=8,'side'=2,'y'=4,'core'=2] {'mx','mz','side'}, dimensions={0} | all-to-all | bytes 262144 | tf_op jit(solution)/shard_map/all_to_all | solution.py:400
  90.8 0.7 copy.14
  (2 shorter events, 0.0 us)
Async XLA Ops:
  0.0 5.7 %copy-start.6 = (f32[1,4,8192]{2,1,0:T(4,128)S(1)}, f32[1,4,8192]{2,1,0:T(4,128)}, u32[]{:S(2)}) copy-start(f32[1,4,8192]{2,1,0:T(4,128)} %param.7) | copy-start | bytes 393220
  0.0 6.5 %collective-permute-start.1 = (f32[4,8192]{1,0:T(4,128)}, f32[4,8192]{1,0:T(4,128)}, u32[]{:S(2)}, u32[]{:S(2)}) collective-permute-start(f32[4,8192]{1,0:T(4,128)} %bitcast.25), channel_id=1, source_target_pairs={{1,2},{3,4},{5,6},{2,1},{4,3},{6,5},{9,10},{11,12},{13,14},{10,9},... | collective-permute-start | bytes 393224 | tf_op jit(solution)/shard_map/ppermute | solution.py:366
  1.4 5.5 %collective-permute-start = (f32[4,8192]{1,0:T(4,128)}, f32[4,8192]{1,0:T(4,128)}, u32[]{:S(2)}, u32[]{:S(2)}) collective-permute-start(f32[4,8192]{1,0:T(4,128)} %bitcast.26), channel_id=1, source_target_pairs={{0,1},{2,3},{4,5},{6,7},{1,0},{3,2},{5,4},{7,6},{8,9},{10,11},{12,... | collective-permute-start | bytes 393224 | tf_op jit(solution)/shard_map/ppermute | solution.py:364
  5.7 0.7 copy-start
  5.7 0.7 copy-start.1
  5.7 0.7 copy-start.2
  5.7 0.7 copy-start.3
  5.7 0.7 copy-start.4
  5.7 0.7 copy-start.5
  50.3 3.1 %collective-permute-start.2 = (f32[24,128]{1,0:T(8,128)S(1)}, f32[24,128]{1,0:T(8,128)S(1)}, u32[]{:S(2)}, u32[]{:S(2)}) collective-permute-start(f32[24,128]{1,0:T(8,128)S(1)} %shard_map.77.own_ref), channel_id=1, source_target_pairs={{0,1},{1,0},{2,3},{3,2},{4,5},{5,4},{6,7},{7,6},{8,9},{9,8},{10,11... | collective-permute-start | bytes 36872 | tf_op jit(solution)/shard_map/ppermute | solution.py:394

commit v9 on v7

--- a/solution.py
+++ b/solution.py
@@ -297,7 +297,7 @@
         (table + (MEMBERS - 1.0)) * (table + (MEMBERS - 1.0)),
         jnp.where(body, 2.0 * table * table, 0.0),
     )
-    scale = jnp.sqrt(jnp.sum(squares, keepdims=True))
+    inverse_scale = lax.rsqrt(jnp.sum(squares, keepdims=True))
     identity, system = (jnp.concatenate([x, x], axis=1) for x in (identity, system))
 
     ensemble = jnp.concatenate(
@@ -308,7 +308,6 @@
         [ensemble - centre, jnp.broadcast_to(cross, (MEMBERS, LANES))], axis=1
     )
 
-    inverse_scale = 1.0 / scale
     root = system * inverse_scale
     inverse_root = 1.5 * identity - 0.5 * root
     root = mm(root, inverse_root)
@@ -319,7 +318,7 @@
             root, inverse_root = both[:MEMBERS], both[MEMBERS:]
     wide = mm(factor, mm(inverse_root, wide))
     drive = wide[:, F * LANES :]
-    gain = math.sqrt(MEMBERS - 1.0) / jnp.sqrt(scale)
+    gain = math.sqrt(MEMBERS - 1.0) * jnp.sqrt(inverse_scale)
     for f in range(F):
         lanes = slice(f * LANES, (f + 1) * LANES)
         anomaly = wide[:, lanes]

time: 90.8 us -> 90.8 us (level)
  no operation moved by 1% of the time
where the time goes in v9:
time: 90.8 us; the launch traced here: 90.3 us
  blocking collectives  77.1 us (85%)
  starting transfers between devices  7.54 us (8%)
  Pallas kernels  3.05 us (3%)
  local copies, waits for them, and re-layouts  1.33 us (1%)
  waiting for transfers between devices  1.22 us (1%)
    all_to_all x2, blocking collectives, exchange(): return lax.all_to_all(blocks, axes, split_axis=0, concat_axis=0, tiled=True)  56.3 us
    all_to_all x1, blocking collectives, per_device(): lax.all_to_all(mixed.reshape(MEMBERS, F, LANES), MEMBER, split_axis=0, co...  20.8 us
    ppermute x1, starting transfers between devices, per_device(): beside = lax.ppermute(own, SPACE, pairs + [(b, a) for a, b in pairs])  4.84 us
    pallas_call x7, Pallas kernels, call(): pl.pallas_call(body, out_shape=jax.ShapeDtypeStruct(out_shape, F32), in_s...  3.05 us
    ppermute x1, starting transfers between devices, per_device(): other = lax.ppermute(table, 'core', [(0, 1), (1, 0)])  1.92 us
  transfers between devices with their start and end apart: 3, of which 2 were waited for; matrix products, arithmetic and copies ran while one was open for 0% of the time, Pallas kernels for 0%

profile of v9, /device:TPU:6, one launch (start us, length us, event | category | flops | bytes accessed | tf_op | source)
XLA Modules:
  0.0 90.3 jit_solution(4173227017200458291)
XLA Ops:
  0.0 0.0 copy-start
  0.0 0.8 collective-permute-start.1
  0.8 4.8 %collective-permute-start = (f32[4,8192]{1,0:T(4,128)}, f32[4,8192]{1,0:T(4,128)S(1)}, u32[]{:S(2)}, u32[]{:S(2)}) collective-permute-start(f32[4,8192]{1,0:T(4,128)} %bitcast.21), channel_id=1, source_target_pairs={{0,1},{2,3},{4,5},{6,7},{1,0},{3,2},{5,4},{7,6},{8,9},{10,11},{12,... | collective-permute-start | bytes 393224 | tf_op jit(solution)/shard_map/ppermute | solution.py:347
  5.6 0.0 copy-start.5
  5.7 0.0 copy-start.6
  5.7 0.0 copy-start.1
  5.7 0.0 copy-start.2
  5.7 0.0 copy-start.3
  5.7 0.0 copy-start.4
  5.7 0.6 copy-done.5
  6.3 0.0 copy-done.6
  6.3 0.0 copy-done.1
  6.4 0.0 copy-done.2
  6.4 0.0 copy-done.3
  6.4 0.0 copy-done.4
  6.4 0.1 shard_map.74.early_ref
  6.5 0.0 copy-done
  6.5 0.2 shard_map.75.own_ref
  6.7 0.0 collective-permute-done.1.across_ref
  6.7 0.1 collective-permute-done.beside_ref
  6.8 0.4 shard_map.76
  7.3 41.4 %all_to_all.15 = f32[64,9,1,128]{3,2,1,0:T(1,128)S(1)} all-to-all(f32[64,9,1,128]{3,2,1,0:T(1,128)S(1)} %bitcast.16), channel_id=1, replica_groups=mesh['mx'=4,'mz'=8,'side'=2,'y'=4,'core'=2] {'mx','mz','side'}, dimensions={0} | all-to-all | bytes 589824 | tf_op jit(solution)/shard_map/all_to_all | solution.py:331
  48.6 0.5 shard_map.77.own_ref
  49.2 1.9 %collective-permute-start.2 = (f32[24,128]{1,0:T(8,128)S(1)}, f32[24,128]{1,0:T(8,128)S(1)}, u32[]{:S(2)}, u32[]{:S(2)}) collective-permute-start(f32[24,128]{1,0:T(8,128)S(1)} %shard_map.77.own_ref), channel_id=1, source_target_pairs={{0,1},{1,0},{2,3},{3,2},{4,5},{5,4},{6,7},{7,6},{8,9},{9,8},{10,11... | collective-permute-start | bytes 36872 | tf_op jit(solution)/shard_map/ppermute | solution.py:377
  51.1 1.1 %collective-permute-done.2.other_ref = f32[24,128]{1,0:T(8,128)S(1)} collective-permute-done((f32[24,128]{1,0:T(8,128)S(1)}, f32[24,128]{1,0:T(8,128)S(1)}, u32[]{:S(2)}, u32[]{:S(2)}) %collective-permute-start.2) | collective-permute-done | bytes 12320 | tf_op jit(solution)/shard_map/ppermute | solution.py:377
  52.3 14.9 %all_to_all.16 = f32[32,17,1,128]{3,2,1,0:T(1,128)S(1)} all-to-all(f32[32,17,1,128]{3,2,1,0:T(1,128)S(1)} %bitcast.17), channel_id=1, replica_groups=mesh['mx'=4,'mz'=8,'side'=2,'y'=4,'core'=2] {'mx','side','y'}, dimensions={0} | all-to-all | bytes 557056 | tf_op jit(solution)/shard_map/all_to_all | solution.py:331
  67.2 1.7 %shard_map.79 = f32[256,128]{1,0:T(8,128)S(1)} custom-call(f32[544,128]{1,0:T(8,128)S(1)} %bitcast.18, f32[576,128]{1,0:T(8,128)S(1)} %bitcast.15), custom_call_target="tpu_custom_call" | custom-call | tf_op jit(solution)/shard_map/pallas_call | solution.py:34
  68.9 20.8 %all_to_all.17 = f32[64,4,128]{2,1,0:T(4,128)S(1)} all-to-all(f32[64,4,128]{2,1,0:T(4,128)S(1)} %bitcast.19), channel_id=1, replica_groups=mesh['mx'=4,'mz'=8,'side'=2,'y'=4,'core'=2] {'mx','mz','side'}, dimensions={0} | all-to-all | bytes 262144 | tf_op jit(solution)/shard_map/all_to_all | solution.py:383
  89.7 0.7 copy.14
  (2 shorter events, 0.0 us)
Async XLA Ops:
  0.0 6.5 %copy-start = (f32[1,4,8192]{2,1,0:T(4,128)S(1)}, f32[1,4,8192]{2,1,0:T(4,128)}, u32[]{:S(2)}) copy-start(f32[1,4,8192]{2,1,0:T(4,128)} %param.7) | copy-start | bytes 393220
  0.0 6.7 %collective-permute-start.1 = (f32[4,8192]{1,0:T(4,128)}, f32[4,8192]{1,0:T(4,128)S(1)}, u32[]{:S(2)}, u32[]{:S(2)}) collective-permute-start(f32[4,8192]{1,0:T(4,128)} %bitcast.20), channel_id=1, source_target_pairs={{1,2},{3,4},{5,6},{2,1},{4,3},{6,5},{9,10},{11,12},{13,14},{10,9},... | collective-permute-start | bytes 393224 | tf_op jit(solution)/shard_map/ppermute | solution.py:349
  0.8 6.0 %collective-permute-start = (f32[4,8192]{1,0:T(4,128)}, f32[4,8192]{1,0:T(4,128)S(1)}, u32[]{:S(2)}, u32[]{:S(2)}) collective-permute-start(f32[4,8192]{1,0:T(4,128)} %bitcast.21), channel_id=1, source_target_pairs={{0,1},{2,3},{4,5},{6,7},{1,0},{3,2},{5,4},{7,6},{8,9},{10,11},{12,... | collective-permute-start | bytes 393224 | tf_op jit(solution)/shard_map/ppermute | solution.py:347
  5.6 0.7 copy-start.5
  5.7 0.7 copy-start.6
  5.7 0.7 copy-start.1
  5.7 0.7 copy-start.2
  5.7 0.7 copy-start.3
  5.7 0.7 copy-start.4
  49.2 3.1 %collective-permute-start.2 = (f32[24,128]{1,0:T(8,128)S(1)}, f32[24,128]{1,0:T(8,128)S(1)}, u32[]{:S(2)}, u32[]{:S(2)}) collective-permute-start(f32[24,128]{1,0:T(8,128)S(1)} %shard_map.77.own_ref), channel_id=1, source_target_pairs={{0,1},{1,0},{2,3},{3,2},{4,5},{5,4},{6,7},{7,6},{8,9},{9,8},{10,11... | collective-permute-start | bytes 36872 | tf_op jit(solution)/shard_map/ppermute | solution.py:377
